TPU v7x, 256 devices: a whole 4x4x8 slice. The times are simulated.
256 devices in a mesh: grp: 8 (over x, z_lo), lat: 32 (over y, z_hi, core).
Axes of the slice: x: 4, y: 4, z: 8 (z_hi: 4, z_lo: 2; z = z_hi * 2 + z_lo), core: 2. Of those that a mesh axis runs over, the one named last changes fastest.
Arguments:
- inputs: bfloat16 [512, 8192], P('lat'), may hold values from -6 to 6
- dec_bias: float32 [8192], replicated, may hold values from -3 to 3
- weight: bfloat16 [32768, 8192], P(('grp', 'lat')), may hold values from -0.0625 to 0.0625
- enc_bias: float32 [32768], P(('grp', 'lat')), may hold values from -1 to 0.5
- first_moment: bfloat16 [32768, 8192], P(('grp', 'lat')), may hold values from -0.15625 to 0.15625
- second_moment: bfloat16 [32768, 8192], P(('grp', 'lat')), may hold values from 9.953976e-06 to 0.0009994507
Outputs:
- update: bfloat16 [32768, 8192], P(('grp', 'lat'))
- new_first: bfloat16 [32768, 8192], P(('grp', 'lat'))
- new_second: bfloat16 [32768, 8192], P(('grp', 'lat'))
All inputs are finite; a program needn't handle non-finite values.
Results may differ from a plain program's by a relative error of at most 0.014.
The roundings to bfloat16 on the way count: a program that leaves them out, or rounds other values in their place, can miss the bound.
Values may be sent and summed in bfloat16 or wider, within the bound.
No kernel may reach another device: no remote copies, remote signals or barrier semaphores. Data moves between devices by JAX's collectives and lax.ppermute only.
A program may use at most 128 MiB of HBM per device.

v0:
```python
import functools

import jax
import jax.numpy as jnp
from jax import lax
from jax.experimental import pallas as pl
from jax.experimental.pallas import tpu as pltpu
from jax.sharding import Mesh, PartitionSpec as P

STEP = 100
BF16 = jnp.bfloat16
F32 = jnp.float32
SIDE = 4
CHUNKS = 2
ORDER = (0, 2, 1, 3)
PLANE = ("x", "y", "c")
Z = ("zh", "zl")
VMEM = pl.BlockSpec(memory_space=pltpu.VMEM)
SMEM = pl.BlockSpec(memory_space=pltpu.SMEM)
LAYOUT = ((0, (0, 1, 2, 3)), (-1, (0, 1, 2, 3)), (1, (0, 1, 2, 3)), (2, (0, 1)), (2, (2, 3)))
PIECES = len(LAYOUT)
WHOLE = tuple((-by, (0, 1, 2, 3)) for by in ORDER)
PARAMS = pltpu.CompilerParams(vmem_limit_bytes=8 * 1024 * 1024)


def plane_pairs(by, last):
    pairs = []
    for x in range(SIDE):
        for y in range(SIDE):
            for c in range(2):
                along_x = (c == 0) == last
                to_x = (x + by) % SIDE if along_x else x
                to_y = y if along_x else (y + by) % SIDE
                pairs.append(((x * SIDE + y) * 2 + c, (to_x * SIDE + to_y) * 2 + c))
    return pairs


def shift(value, by, last):
    return lax.ppermute(value, PLANE, plane_pairs(by, last))


def swap(value):
    return lax.ppermute(value, "c", [(0, 1), (1, 0)])


def spread(piece, last):
    return [piece] + [shift(piece, by, last) for by in ORDER[1:]]


def relay(piece):
    behind, ahead = shift(piece, 1, True), shift(piece, SIDE - 1, True)
    return [piece, behind, ahead, shift(behind[:2], 1, True), shift(ahead[2:], SIDE - 1, True)]


def fold(own, up, down, far_up, far_down):
    from_behind, from_ahead = shift(far_up, 1, True), shift(far_down, SIDE - 1, True)
    up = jnp.concatenate([up[:2] + from_behind, up[2:]], 0)
    down = jnp.concatenate([down[:2], down[2:] + from_ahead], 0)
    from_behind, from_ahead = shift(up, 1, True), shift(down, SIDE - 1, True)
    return (own.astype(F32) + from_behind.astype(F32) + from_ahead.astype(F32)).astype(BF16)


def corner(me, away, j, thick, part):
    last = (me[1] + (away + SIDE)) % SIDE
    first = (me[2] + (SIDE - (j % 2 * 2 + j // 2))) % SIDE
    row, column = jnp.where(me[0] == 0, first, last), jnp.where(me[0] == 0, last, first)
    return pl.multiple_of(row * thick, thick), pl.multiple_of(column * part, part)


def project_kernel(me, weight, extra, lift, *refs, centre):
    layout = LAYOUT if centre else WHOLE
    pieces, (laid, product) = refs[: len(layout)], refs[-2:]
    thick, part = pieces[0].shape[1:]
    for piece, (away, blocks) in zip(pieces, layout):

        def place(i, carry, piece=piece, away=away, begin=blocks[0]):
            row, column = corner(me, away, begin + i, thick, part)
            block = piece[i]
            if centre:
                block = (block.astype(F32) - extra[:, pl.ds(column, part)]).astype(BF16)
            laid[pl.ds(row, thick), pl.ds(column, part)] = block
            return carry

        lax.fori_loop(0, len(blocks), place, 0)
    product[...] = jnp.broadcast_to(lift[...], product.shape) if centre else jnp.zeros_like(product)

    def multiply(q, carry):
        columns = pl.ds(pl.multiple_of(q * part, part), part)
        product[...] += lax.dot_general(
            laid[:, columns], weight[:, columns], (((1,), (1,)), ((), ())), preferred_element_type=F32
        )
        return carry

    lax.fori_loop(0, SIDE, multiply, 0)


def project(me, weight, extra, lift, pieces, centre, after=()):
    thick, part = pieces[0].shape[1:]
    rows, width = thick * SIDE, part * SIDE
    args = (me, weight, extra, lift, *pieces, *after)
    return pl.pallas_call(
        functools.partial(project_kernel, centre=centre),
        out_shape=(jax.ShapeDtypeStruct((rows, width), BF16), jax.ShapeDtypeStruct((rows, weight.shape[0]), F32)),
        in_specs=[SMEM] + [VMEM] * (3 + len(pieces)) + [pl.BlockSpec(memory_space=pl.ANY)] * len(after),
        out_specs=(VMEM, VMEM),
        compiler_params=PARAMS,
        cost_estimate=pl.CostEstimate(
            flops=2 * rows * width * weight.shape[0], bytes_accessed=4 * rows * width, transcendentals=0
        ),
    )(*args)


def join(own, other, latents):
    return jnp.concatenate([own[:, :latents] + other[:, latents:], own[:, latents:] + other[:, :latents]], 1)


def recon_kernel(me, own, other, weight, preact, flat, *refs):
    blocks, (activity, laid) = refs[:PIECES], refs[PIECES:]
    _, thick, part = blocks[0].shape
    value = join(own[...], other[...], own.shape[1] // 2)
    preact[...] = value
    positive = jnp.maximum(value, 0.0)
    activity[...] = positive.astype(BF16)
    flat[...] = positive.T.astype(BF16)

    def multiply(q, carry):
        columns = pl.ds(pl.multiple_of(q * part, part), part)
        laid[:, columns] = jnp.dot(activity[...], weight[:, columns], preferred_element_type=F32).astype(BF16)
        return carry

    lax.fori_loop(0, SIDE, multiply, 0)
    for piece, (away, wanted) in zip(blocks, LAYOUT):

        def take(i, carry, piece=piece, away=away, begin=wanted[0]):
            row, column = corner(me, -away, begin + i, thick, part)
            piece[i] = laid[pl.ds(row, thick), pl.ds(column, part)]
            return carry

        lax.fori_loop(0, len(wanted), take, 0)


def recon(me, own, other, weight):
    rows, wide = own.shape
    width = weight.shape[1]
    args = (me, own, other, weight)
    shapes = [jax.ShapeDtypeStruct((rows, wide), F32), jax.ShapeDtypeStruct((wide, rows), BF16)]
    for _, wanted in LAYOUT:
        shapes.append(jax.ShapeDtypeStruct((len(wanted), rows // SIDE, width // SIDE), BF16))
    return pl.pallas_call(
        recon_kernel,
        out_shape=tuple(shapes),
        in_specs=[SMEM] + [VMEM] * 3,
        out_specs=(VMEM,) * len(shapes),
        scratch_shapes=[pltpu.VMEM((rows, wide), BF16), pltpu.VMEM((rows, width), BF16)],
        compiler_params=PARAMS,
        cost_estimate=pl.CostEstimate(flops=2 * rows * wide * width, bytes_accessed=4 * rows * width, transcendentals=0),
    )(*args)


def error_kernel(me, parts, source, decoder, out):
    thin, part = out.shape[1:]
    x = jnp.where(me[0] == 0, me[1], me[2])
    rows = pl.ds(pl.multiple_of(me[3] * thin, thin), thin)
    value = jnp.sum(parts[...].astype(F32), 0) + decoder[:, pl.ds(pl.multiple_of(x * part, part), part)]
    value = (value - source[rows, :].astype(F32)).astype(BF16)
    for k in range(out.shape[0]):
        out[k] = value


def find_error(me, parts, source, decoder):
    return pl.pallas_call(
        error_kernel,
        out_shape=jax.ShapeDtypeStruct(parts.shape, BF16),
        in_specs=[SMEM] + [VMEM] * 3,
        out_specs=VMEM,
        compiler_params=PARAMS,
        cost_estimate=pl.CostEstimate(flops=10 * parts.size, bytes_accessed=4 * parts.size, transcendentals=0),
    )(me, parts, source, decoder)


def gradient_kernel(own, other, preact, flat, error, centered, *refs, chunk, final):
    slope = refs[-1]
    latents = preact.shape[1] // 2
    value = jnp.where(preact[...] > 0, join(own[...], other[...], latents), 0.0)
    slope[...] = value.T.astype(BF16)

    def step(j, carry):
        columns = pl.ds(pl.multiple_of(j * chunk, chunk), chunk)
        total = jnp.dot(flat[...], error[:, columns], preferred_element_type=F32)
        total += jnp.dot(slope[...], centered[:, columns], preferred_element_type=F32)
        if final:
            before, mine, theirs = refs[:3]
            total += before[:, columns]
            mine[:, columns] = total[:latents]
            theirs[:, columns] = total[latents:].astype(BF16)
        else:
            refs[0][:, columns] = total
        return carry

    lax.fori_loop(0, error.shape[1] // chunk, step, 0)


def gradient(args, before, chunk=1024):
    flat, error = args[3], args[4]
    wide, width = flat.shape[0], error.shape[1]
    if before is None:
        shapes = jax.ShapeDtypeStruct((wide, width), F32)
    else:
        args = args + (before,)
        shapes = (jax.ShapeDtypeStruct((wide // 2, width), F32), jax.ShapeDtypeStruct((wide // 2, width), BF16))
    return pl.pallas_call(
        functools.partial(gradient_kernel, chunk=chunk, final=before is not None),
        out_shape=shapes,
        in_specs=[VMEM] * len(args),
        out_specs=jax.tree.map(lambda _: VMEM, shapes),
        scratch_shapes=[pltpu.VMEM(flat.shape, BF16)],
        compiler_params=PARAMS,
        cost_estimate=pl.CostEstimate(flops=4 * flat.size * width, bytes_accessed=12 * error.size, transcendentals=0),
    )(*args)


def adam_kernel(at, gradient_ref, first_ref, second_ref, *refs, rows):
    update_out, first_out, second_out = refs[-3:]
    gradient = gradient_ref[...].astype(F32) * (1.0 / rows)
    first = 0.9 * first_ref[...].astype(F32) + 0.1 * gradient
    second = 0.999 * second_ref[...].astype(F32) + 0.001 * gradient * gradient
    update = first * (1.0 / (1.0 - 0.9**STEP)) / (jnp.sqrt(second * (1.0 / (1.0 - 0.999**STEP))) + 1e-08)
    update_out[...] = update.astype(BF16)
    first_out[...] = first.astype(BF16)
    second_out[...] = second.astype(BF16)


def adam(at, gradient, first_moment, second_moment, outs, rows, chunk=1024):
    latents, width = gradient.shape
    count = width // chunk
    here = pl.BlockSpec((latents, chunk), lambda i, at: (0, i))
    there = pl.BlockSpec((latents, chunk), lambda i, at: (0, at[0] * count + i))
    held = [pl.BlockSpec(memory_space=pl.ANY)] * len(outs)
    return pl.pallas_call(
        functools.partial(adam_kernel, rows=rows),
        out_shape=(jax.ShapeDtypeStruct(first_moment.shape, BF16),) * 3,
        grid_spec=pltpu.PrefetchScalarGridSpec(
            num_scalar_prefetch=1,
            grid=(count,),
            in_specs=[here, there, there] + held,
            out_specs=(there,) * 3,
        ),
        input_output_aliases={4 + i: i for i in range(len(outs))},
        compiler_params=PARAMS,
        cost_estimate=pl.CostEstimate(flops=20 * gradient.size, bytes_accessed=14 * gradient.size, transcendentals=0),
    )(at, gradient, first_moment, second_moment, *outs)


def body(inputs, dec_bias, weight, enc_bias, first_moment, second_moment):
    latents, width = weight.shape
    half = width // 2
    part = half // SIDE
    x, y, c = lax.axis_index("x"), lax.axis_index("y"), lax.axis_index("c")
    zh, z = lax.axis_index("zh"), lax.axis_index(Z)
    last_me, first_me = jnp.where(c == 0, x, y), jnp.where(c == 0, y, x)
    me = jnp.stack([c, last_me, first_me, z]).astype(jnp.int32)

    kept = lax.dynamic_slice_in_dim(inputs, c * half + x * part, part, 1)
    given = swap(lax.dynamic_slice_in_dim(inputs, (1 - c) * half + x * part, part, 1))
    both = jnp.concatenate([jnp.where(c == 0, kept, given), jnp.where(c == 0, given, kept)], 0)
    count = both.shape[0]
    block = lax.dynamic_update_slice_in_dim(jnp.zeros((SIDE * count, part), BF16), both, zh * count, 0)
    for by in ORDER[1:]:
        arrived = lax.ppermute(both, "zh", [(i, (i + by) % SIDE) for i in range(SIDE)])
        block = lax.dynamic_update_slice_in_dim(block, arrived, (zh - by) % SIDE * count, 0)
    source = block
    split = source.shape[0] // CHUNKS
    gathered = spread(source, False)

    pair = jnp.concatenate(
        [lax.dynamic_slice_in_dim(rows_held, c * half, half, 1) for rows_held in (weight, swap(weight))], 0
    )
    decoder = lax.dynamic_slice_in_dim(dec_bias, c * half, half, 0)[None, :]
    lift = jnp.concatenate([enc_bias, jnp.zeros_like(enc_bias)])[None, :]
    rows = source.shape[0] * SIDE
    thin = source.shape[0] // 8

    def fan(gathered, send):
        return [send(jnp.stack([g[k * split : (k + 1) * split] for g in gathered])) for k in chunks]

    chunks = range(CHUNKS)
    pieces = fan(gathered, relay)
    ahead, made = [], []
    for k in chunks:
        ahead.append(project(me, pair, decoder, lift, pieces[k], True))
        made.append(recon(me, ahead[k][1], swap(ahead[k][1]), pair))
    blocks = jnp.concatenate([fold(*made[k][2:]) for k in chunks], 1)
    strip = blocks[0].astype(F32)
    for by in ORDER[1:]:
        strip = strip + shift(blocks[ORDER.index(SIDE - by)], by, False).astype(F32)
    parts = lax.all_to_all(strip.astype(BF16).reshape(8, thin, part), Z, 0, 0, tiled=True)
    error = find_error(me, parts, source, decoder)
    error = lax.all_to_all(error, Z, 0, 0, tiled=True)
    pieces = fan(spread(error.reshape(-1, part), False), lambda piece: spread(piece, True))
    total = None
    for k in chunks:
        after = () if total is None else (total,)
        laid, own = project(me, pair, decoder, lift, pieces[k], False, after)
        total = gradient((own, swap(own), made[k][0], made[k][1], laid, ahead[k][0]), total)
    mine, theirs = total
    arrived = swap(theirs)
    at = c.astype(jnp.int32)[None]
    outs = adam(at, mine, first_moment, second_moment, (), rows)
    return tuple(adam(1 - at, arrived, first_moment, second_moment, outs, rows))


def solution(mesh):
    fine = Mesh(mesh.devices.reshape(4, 2, 4, 4, 2), ("x", "zl", "y", "zh", "c"))
    lat = ("y", "zh", "c")
    everything = ("x", "zl", "y", "zh", "c")
    return jax.shard_map(
        body,
        mesh=fine,
        in_specs=(P(lat, None), P(), P(everything, None), P(everything), P(everything, None), P(everything, None)),
        out_specs=(P(everything, None),) * 3,
        check_vma=False,
    )
```

profile of v0, /device:TPU:1, one launch (start us, length us, event | category | flops | bytes accessed | tf_op | source)
XLA Modules:
  0.0 185.9 jit_solution(16738100176915463742)
XLA Ops:
  1.4 3.2 %collective-permute-start.1 = (bf16[16,1024]{1,0:T(8,128)(2,1)S(1)}, bf16[16,1024]{1,0:T(8,128)(2,1)S(1)}, u32[]{:S(2)}, u32[]{:S(2)}) collective-permute-start(bf16[16,1024]{1,0:T(8,128)(2,1)S(1)} %constant_dynamic-slice_fusion), channel_id=1, source_target_pairs={{0,1},{1,0},{2,3},{3,2},{4,5},{5,4},{6,7},{7,6},{8,9},{9,8},{10,11... | collective-permute-start | bytes 98312 | tf_op jit(solution)/shard_map/ppermute | solution.py:43
  6.3 5.3 %collective-permute-start.2 = (bf16[32,1024]{1,0:T(8,128)(2,1)S(1)}, bf16[32,1024]{1,0:T(8,128)(2,1)S(1)}, u32[]{:S(2)}, u32[]{:S(2)}) collective-permute-start(bf16[32,1024]{1,0:T(8,128)(2,1)S(1)} %get-tuple-element.86), channel_id=1, source_target_pairs={{0,4},{2,6},{4,0},{6,2},{1,5},{3,7},{5,1},{7,3},{8,12},{10,14},{12... | collective-permute-start | bytes 196616 | tf_op jit(solution)/shard_map/ppermute | solution.py:269
  13.4 2.4 %collective-permute-start.4 = (bf16[32,1024]{1,0:T(8,128)(2,1)S(1)}, bf16[32,1024]{1,0:T(8,128)(2,1)S(1)}, u32[]{:S(2)}, u32[]{:S(2)}) collective-permute-start(bf16[32,1024]{1,0:T(8,128)(2,1)S(1)} %get-tuple-element.86), channel_id=1, source_target_pairs={{0,6},{2,0},{4,2},{6,4},{1,7},{3,1},{5,3},{7,5},{8,14},{10,8},{12,... | collective-permute-start | bytes 196616 | tf_op jit(solution)/shard_map/ppermute | solution.py:269
  15.8 3.0 %collective-permute-done.3 = bf16[32,1024]{1,0:T(8,128)(2,1)S(1)} collective-permute-done((bf16[32,1024]{1,0:T(8,128)(2,1)S(1)}, bf16[32,1024]{1,0:T(8,128)(2,1)S(1)}, u32[]{:S(2)}, u32[]{:S(2)}) %collective-permute-start.3) | collective-permute-done | bytes 65568 | tf_op jit(solution)/shard_map/ppermute | solution.py:269
  18.9 2.8 %collective-permute-start.5 = (bf16[128,1024]{1,0:T(8,128)(2,1)S(1)}, bf16[128,1024]{1,0:T(8,128)(2,1)S(1)}, u32[]{:S(2)}, u32[]{:S(2)}) collective-permute-start(bf16[128,1024]{1,0:T(8,128)(2,1)S(1)} %constant_dynamic-update-slice_fusion.source), channel_id=1, source_target_pairs={{0,16},{1,129},{8,24},{9,137},{16,0},{17,145},{24,8},{25,153},{64,... | collective-permute-start | bytes 786440 | tf_op jit(solution)/shard_map/ppermute | solution.py:39
  22.0 2.4 %collective-permute-start.7 = (bf16[128,1024]{1,0:T(8,128)(2,1)S(1)}, bf16[128,1024]{1,0:T(8,128)(2,1)S(1)}, u32[]{:S(2)}, u32[]{:S(2)}) collective-permute-start(bf16[128,1024]{1,0:T(8,128)(2,1)S(1)} %constant_dynamic-update-slice_fusion.source), channel_id=1, source_target_pairs={{0,24},{1,193},{8,0},{9,201},{16,8},{17,209},{24,16},{25,217},{64,... | collective-permute-start | bytes 786440 | tf_op jit(solution)/shard_map/ppermute | solution.py:39
  24.4 1.6 collective-permute-done.5
  26.0 2.8 %collective-permute-done.6 = bf16[128,1024]{1,0:T(8,128)(2,1)S(1)} collective-permute-done((bf16[128,1024]{1,0:T(8,128)(2,1)S(1)}, bf16[128,1024]{1,0:T(8,128)(2,1)S(1)}, u32[]{:S(2)}, u32[]{:S(2)}) %collective-permute-start.6) | collective-permute-done | bytes 262176 | tf_op jit(solution)/shard_map/ppermute | solution.py:39
  29.0 1.4 collective-permute-start.17
  30.4 1.5 collective-permute-start.18
  32.1 2.7 %collective-permute-start.9 = (bf16[4,64,1024]{2,1,0:T(8,128)(2,1)S(1)}, bf16[4,64,1024]{2,1,0:T(8,128)(2,1)S(1)}, u32[]{:S(2)}, u32[]{:S(2)}) collective-permute-start(bf16[4,64,1024]{2,1,0:T(8,128)(2,1)S(1)} %pad_maximum_fusion.1.refs_0_), channel_id=1, source_target_pairs={{0,192},{1,25},{8,200},{9,1},{16,208},{17,9},{24,216},{25,17},{64,... | collective-permute-start | bytes 1572872 | tf_op jit(solution)/shard_map/ppermute | solution.py:39
  36.1 2.5 %collective-permute-done.17.refs_1_ = bf16[4,64,1024]{2,1,0:T(8,128)(2,1)S(1)} collective-permute-done((bf16[4,64,1024]{2,1,0:T(8,128)(2,1)S(1)}, bf16[4,64,1024]{2,1,0:T(8,128)(2,1)S(1)}, u32[]{:S(2)}, u32[]{:S(2)}) %collective-permute-start.17) | collective-permute-done | bytes 524320 | tf_op jit(solution)/shard_map/ppermute | solution.py:39
  38.8 2.7 %collective-permute-start.20 = (bf16[2,64,1024]{2,1,0:T(8,128)(2,1)S(1)}, bf16[2,64,1024]{2,1,0:T(8,128)(2,1)S(1)}, u32[]{:S(2)}, u32[]{:S(2)}) collective-permute-start(bf16[2,64,1024]{2,1,0:T(8,128)(2,1)S(1)} %slice.141), channel_id=1, source_target_pairs={{0,192},{1,25},{8,200},{9,1},{16,208},{17,9},{24,216},{25,17},{64,... | collective-permute-start | bytes 786440 | tf_op jit(solution)/shard_map/ppermute | solution.py:39
  41.5 2.7 %collective-permute-done.8.refs_1_ = bf16[4,64,1024]{2,1,0:T(8,128)(2,1)S(1)} collective-permute-done((bf16[4,64,1024]{2,1,0:T(8,128)(2,1)S(1)}, bf16[4,64,1024]{2,1,0:T(8,128)(2,1)S(1)}, u32[]{:S(2)}, u32[]{:S(2)}) %collective-permute-start.8) | collective-permute-done | bytes 524320 | tf_op jit(solution)/shard_map/ppermute | solution.py:39
  44.4 2.9 %collective-permute-start.11 = (bf16[2,64,1024]{2,1,0:T(8,128)(2,1)S(1)}, bf16[2,64,1024]{2,1,0:T(8,128)(2,1)S(1)}, u32[]{:S(2)}, u32[]{:S(2)}) collective-permute-start(bf16[2,64,1024]{2,1,0:T(8,128)(2,1)S(1)} %slice.135), channel_id=1, source_target_pairs={{0,192},{1,25},{8,200},{9,1},{16,208},{17,9},{24,216},{25,17},{64,... | collective-permute-start | bytes 786440 | tf_op jit(solution)/shard_map/ppermute | solution.py:39
  48.9 2.5 %shard_map.87 = (bf16[256,4096]{1,0:T(8,128)(2,1)S(1)}, f32[256,256]{1,0:T(8,128)S(1)}) custom-call(s32[4]{0:T(128)S(1)} %pad_add_fusion.me, bf16[256,4096]{1,0:T(8,128)(2,1)S(1)} %pad_maximum_fusion.weight, f32[1,4096]{1,0:T(1,128)S(1)} %bitcast.49, f32[1,256]{1,0:T(1,128)S(1)} %bitcast.54, bf16[4,64,1024]{2,1,0:T(8,128)(2,1)S(1)} %pad_maximum_fusion.4.refs_0_, ...), custom_call_target="tpu_custom_call" | custom-call | flops 536870912 | bytes 4194304 | tf_op jit(solution)/shard_map/pallas_call | solution.py:101
  51.4 4.0 %collective-permute-start.21 = (f32[256,256]{1,0:T(8,128)S(1)}, f32[256,256]{1,0:T(8,128)S(1)}, u32[]{:S(2)}, u32[]{:S(2)}) collective-permute-start(f32[256,256]{1,0:T(8,128)S(1)} %get-tuple-element.36.own), channel_id=1, source_target_pairs={{0,1},{1,0},{2,3},{3,2},{4,5},{5,4},{6,7},{7,6},{8,9},{9,8},{10,11... | collective-permute-start | bytes 786440 | tf_op jit(solution)/shard_map/ppermute | solution.py:43
  55.4 2.5 %shard_map.85 = (bf16[256,4096]{1,0:T(8,128)(2,1)S(1)}, f32[256,256]{1,0:T(8,128)S(1)}) custom-call(s32[4]{0:T(128)S(1)} %pad_add_fusion.me, bf16[256,4096]{1,0:T(8,128)(2,1)S(1)} %pad_maximum_fusion.weight, f32[1,4096]{1,0:T(1,128)S(1)} %bitcast.50, f32[1,256]{1,0:T(1,128)S(1)} %bitcast.55, bf16[4,64,1024]{2,1,0:T(8,128)(2,1)S(1)} %pad_maximum_fusion.1.refs_0_, ...), custom_call_target="tpu_custom_call" | custom-call | flops 536870912 | bytes 4194304 | tf_op jit(solution)/shard_map/pallas_call | solution.py:101
  58.1 2.3 %shard_map.88 = (f32[256,256]{1,0:T(8,128)S(1)}, bf16[256,256]{1,0:T(8,128)(2,1)S(1)}, bf16[4,64,1024]{2,1,0:T(8,128)(2,1)S(1)}, bf16[4,64,1024]{2,1,0:T(8,128)(...) custom-call(s32[4]{0:T(128)S(1)} %pad_add_fusion.me, ...), custom_call_target="tpu_custom_call" | custom-call | flops 536870912 | bytes 4194304 | tf_op jit(solution)/shard_map/pallas_call | solution.py:149
  61.6 1.6 collective-permute-start.24
  63.3 2.3 %shard_map.86 = (f32[256,256]{1,0:T(8,128)S(1)}, bf16[256,256]{1,0:T(8,128)(2,1)S(1)}, bf16[4,64,1024]{2,1,0:T(8,128)(2,1)S(1)}, bf16[4,64,1024]{2,1,0:T(8,128)(...) custom-call(s32[4]{0:T(128)S(1)} %pad_add_fusion.me, ...), custom_call_target="tpu_custom_call" | custom-call | flops 536870912 | bytes 4194304 | tf_op jit(solution)/shard_map/pallas_call | solution.py:149
  65.7 2.7 %collective-permute-start.15 = (bf16[2,64,1024]{2,1,0:T(8,128)(2,1)S(1)}, bf16[2,64,1024]{2,1,0:T(8,128)(2,1)S(1)}, u32[]{:S(2)}, u32[]{:S(2)}) collective-permute-start(bf16[2,64,1024]{2,1,0:T(8,128)(2,1)S(1)} %get-tuple-element.35), channel_id=1, source_target_pairs={{0,192},{1,25},{8,200},{9,1},{16,208},{17,9},{24,216},{25,17},{64,... | collective-permute-start | bytes 786440 | tf_op jit(solution)/shard_map/ppermute | solution.py:39
  68.7 2.7 %collective-permute-start.25 = (bf16[4,64,1024]{2,1,0:T(8,128)(2,1)S(1)}, bf16[4,64,1024]{2,1,0:T(8,128)(2,1)S(1)}, u32[]{:S(2)}, u32[]{:S(2)}) collective-permute-start(bf16[4,64,1024]{2,1,0:T(8,128)(2,1)S(1)} %pad_maximum_fusion.6), channel_id=1, source_target_pairs={{0,192},{1,25},{8,200},{9,1},{16,208},{17,9},{24,216},{25,17},{64,... | collective-permute-start | bytes 1572872 | tf_op jit(solution)/shard_map/ppermute | solution.py:39
  72.7 2.7 %collective-permute-start.16 = (bf16[4,64,1024]{2,1,0:T(8,128)(2,1)S(1)}, bf16[4,64,1024]{2,1,0:T(8,128)(2,1)S(1)}, u32[]{:S(2)}, u32[]{:S(2)}) collective-permute-start(bf16[4,64,1024]{2,1,0:T(8,128)(2,1)S(1)} %pad_maximum_fusion.3), channel_id=1, source_target_pairs={{0,192},{1,25},{8,200},{9,1},{16,208},{17,9},{24,216},{25,17},{64,... | collective-permute-start | bytes 1572872 | tf_op jit(solution)/shard_map/ppermute | solution.py:39
  75.5 2.6 %collective-permute-done.23 = bf16[4,64,1024]{2,1,0:T(8,128)(2,1)S(1)} collective-permute-done((bf16[4,64,1024]{2,1,0:T(8,128)(2,1)S(1)}, bf16[4,64,1024]{2,1,0:T(8,128)(2,1)S(1)}, u32[]{:S(2)}, u32[]{:S(2)}) %collective-permute-start.23) | collective-permute-done | bytes 524320 | tf_op jit(solution)/shard_map/ppermute | solution.py:39
  78.4 5.3 %collective-permute-done.14 = bf16[4,64,1024]{2,1,0:T(8,128)(2,1)S(1)} collective-permute-done((bf16[4,64,1024]{2,1,0:T(8,128)(2,1)S(1)}, bf16[4,64,1024]{2,1,0:T(8,128)(2,1)S(1)}, u32[]{:S(2)}, u32[]{:S(2)}) %collective-permute-start.14) | collective-permute-done | bytes 524320 | tf_op jit(solution)/shard_map/ppermute | solution.py:39
  84.1 1.5 collective-permute-start.26
  85.5 2.3 %collective-permute-start.27 = (bf16[128,1024]{1,0:T(8,128)(2,1)S(1)}, bf16[128,1024]{1,0:T(8,128)(2,1)S(1)}, u32[]{:S(2)}, u32[]{:S(2)}) collective-permute-start(bf16[128,1024]{1,0:T(8,128)(2,1)S(1)} %get-tuple-element.59), channel_id=1, source_target_pairs={{0,8},{1,65},{8,16},{9,73},{16,24},{17,81},{24,0},{25,89},{64,72},... | collective-permute-start | bytes 786440 | tf_op jit(solution)/shard_map/ppermute | solution.py:39
  88.2 3.0 %collective-permute-done.26 = bf16[128,1024]{1,0:T(8,128)(2,1)S(1)} collective-permute-done((bf16[128,1024]{1,0:T(8,128)(2,1)S(1)}, bf16[128,1024]{1,0:T(8,128)(2,1)S(1)}, u32[]{:S(2)}, u32[]{:S(2)}) %collective-permute-start.26) | collective-permute-done | bytes 262176 | tf_op jit(solution)/shard_map/ppermute | solution.py:39
  91.2 2.8 %collective-permute-done.27 = bf16[128,1024]{1,0:T(8,128)(2,1)S(1)} collective-permute-done((bf16[128,1024]{1,0:T(8,128)(2,1)S(1)}, bf16[128,1024]{1,0:T(8,128)(2,1)S(1)}, u32[]{:S(2)}, u32[]{:S(2)}) %collective-permute-start.27) | collective-permute-done | bytes 262176 | tf_op jit(solution)/shard_map/ppermute | solution.py:39
  94.9 14.0 %all_to_all.10.parts = bf16[8,16,1024]{2,1,0:T(8,128)(2,1)S(1)} all-to-all(bf16[8,16,1024]{2,1,0:T(8,128)(2,1)S(1)} %bitcast.61), channel_id=1, replica_groups=mesh['x'=4,'zl'=2,'y'=4,'zh'=4,'c'=2] {'zh','zl'}, dimensions={0} | all-to-all | bytes 524288 | tf_op jit(solution)/shard_map/all_to_all | solution.py:296
  109.5 11.7 %all_to_all.11 = bf16[8,16,1024]{2,1,0:T(8,128)(2,1)S(1)} all-to-all(bf16[8,16,1024]{2,1,0:T(8,128)(2,1)S(1)} %shard_map.89), channel_id=1, replica_groups=mesh['x'=4,'zl'=2,'y'=4,'zh'=4,'c'=2] {'zh','zl'}, dimensions={0} | all-to-all | bytes 524288 | tf_op jit(solution)/shard_map/all_to_all | solution.py:298
  122.0 2.3 %collective-permute-start.30 = (bf16[128,1024]{1,0:T(8,128)(2,1)S(1)}, bf16[128,1024]{1,0:T(8,128)(2,1)S(1)}, u32[]{:S(2)}, u32[]{:S(2)}) collective-permute-start(bf16[128,1024]{1,0:T(8,128)(2,1)S(1)} %bitcast.59), channel_id=1, source_target_pairs={{0,8},{1,65},{8,16},{9,73},{16,24},{17,81},{24,0},{25,89},{64,72},... | collective-permute-start | bytes 786440 | tf_op jit(solution)/shard_map/ppermute | solution.py:39
  124.7 3.3 %collective-permute-done.29 = bf16[128,1024]{1,0:T(8,128)(2,1)S(1)} collective-permute-done((bf16[128,1024]{1,0:T(8,128)(2,1)S(1)}, bf16[128,1024]{1,0:T(8,128)(2,1)S(1)}, u32[]{:S(2)}, u32[]{:S(2)}) %collective-permute-start.29) | collective-permute-done | bytes 262176 | tf_op jit(solution)/shard_map/ppermute | solution.py:39
  128.1 2.7 %collective-permute-done.30 = bf16[128,1024]{1,0:T(8,128)(2,1)S(1)} collective-permute-done((bf16[128,1024]{1,0:T(8,128)(2,1)S(1)}, bf16[128,1024]{1,0:T(8,128)(2,1)S(1)}, u32[]{:S(2)}, u32[]{:S(2)}) %collective-permute-start.30) | collective-permute-done | bytes 262176 | tf_op jit(solution)/shard_map/ppermute | solution.py:39
  132.4 2.5 %collective-permute-start.36 = (bf16[4,64,1024]{2,1,0:T(8,128)(2,1)S(1)}, bf16[4,64,1024]{2,1,0:T(8,128)(2,1)S(1)}, u32[]{:S(2)}, u32[]{:S(2)}) collective-permute-start(bf16[4,64,1024]{2,1,0:T(8,128)(2,1)S(1)} %pad_maximum_fusion.8.refs_0_), channel_id=1, source_target_pairs={{0,64},{1,9},{8,72},{9,17},{16,80},{17,25},{24,88},{25,1},{64,128}... | collective-permute-start | bytes 1572872 | tf_op jit(solution)/shard_map/ppermute | solution.py:39
  135.1 1.7 collective-permute-start.32
  136.9 5.3 %collective-permute-done.35.refs_1_ = bf16[4,64,1024]{2,1,0:T(8,128)(2,1)S(1)} collective-permute-done((bf16[4,64,1024]{2,1,0:T(8,128)(2,1)S(1)}, bf16[4,64,1024]{2,1,0:T(8,128)(2,1)S(1)}, u32[]{:S(2)}, u32[]{:S(2)}) %collective-permute-start.35) | collective-permute-done | bytes 524320 | tf_op jit(solution)/shard_map/ppermute | solution.py:39
  142.2 2.4 %collective-permute-start.34 = (bf16[4,64,1024]{2,1,0:T(8,128)(2,1)S(1)}, bf16[4,64,1024]{2,1,0:T(8,128)(2,1)S(1)}, u32[]{:S(2)}, u32[]{:S(2)}) collective-permute-start(bf16[4,64,1024]{2,1,0:T(8,128)(2,1)S(1)} %pad_maximum_fusion.7.refs_0_), channel_id=1, source_target_pairs={{0,192},{1,25},{8,200},{9,1},{16,208},{17,9},{24,216},{25,17},{64,... | collective-permute-start | bytes 1572872 | tf_op jit(solution)/shard_map/ppermute | solution.py:39
  144.6 3.1 %collective-permute-done.36.refs_2_ = bf16[4,64,1024]{2,1,0:T(8,128)(2,1)S(1)} collective-permute-done((bf16[4,64,1024]{2,1,0:T(8,128)(2,1)S(1)}, bf16[4,64,1024]{2,1,0:T(8,128)(2,1)S(1)}, u32[]{:S(2)}, u32[]{:S(2)}) %collective-permute-start.36) | collective-permute-done | bytes 524320 | tf_op jit(solution)/shard_map/ppermute | solution.py:39
  147.7 2.3 %shard_map.90 = (bf16[256,4096]{1,0:T(8,128)(2,1)S(1)}, f32[256,256]{1,0:T(8,128)S(1)}) custom-call(s32[4]{0:T(128)S(1)} %pad_add_fusion.me, bf16[256,4096]{1,0:T(8,128)(2,1)S(1)} %pad_maximum_fusion.weight, f32[1,4096]{1,0:T(1,128)S(1)} %bitcast.52, f32[1,256]{1,0:T(1,128)S(1)} %bitcast.56, bf16[4,64,1024]{2,1,0:T(8,128)(2,1)S(1)} %pad_maximum_fusion.8.refs_0_, ...), custom_call_target="tpu_custom_call" | custom-call | flops 536870912 | bytes 4194304 | tf_op jit(solution)/shard_map/pallas_call | solution.py:101
  150.1 14.2 %collective-permute-start.38 = (f32[256,256]{1,0:T(8,128)S(1)}, f32[256,256]{1,0:T(8,128)S(1)}, u32[]{:S(2)}, u32[]{:S(2)}) collective-permute-start(f32[256,256]{1,0:T(8,128)S(1)} %get-tuple-element.42.own), channel_id=1, source_target_pairs={{0,1},{1,0},{2,3},{3,2},{4,5},{5,4},{6,7},{7,6},{8,9},{9,8},{10,11... | collective-permute-start | bytes 786440 | tf_op jit(solution)/shard_map/ppermute | solution.py:43
  165.4 1.9 %shard_map.91.refs_4_.refs_0_ = f32[256,4096]{1,0:T(8,128)S(1)} custom-call(f32[256,256]{1,0:T(8,128)S(1)} %get-tuple-element.42.own, f32[256,256]{1,0:T(8,128)S(1)} %collective-permute-done.38.other, f32[256,256]{1,0:T(8,128)S(1)} %get-tuple-element.43.preact, bf16[256,256]{1,0:T(8,128)(2,1)S(1)} %get-tuple-element.44.flat, ...), custom_call_target="tpu_custom_call" | custom-call | flops 1073741824 | bytes 12582912 | tf_op jit(solution)/shard_map/pallas_call | solution.py:211
  167.3 2.3 %shard_map.92 = (bf16[256,4096]{1,0:T(8,128)(2,1)S(1)}, f32[256,256]{1,0:T(8,128)S(1)}) custom-call(s32[4]{0:T(128)S(1)} %pad_add_fusion.me, bf16[256,4096]{1,0:T(8,128)(2,1)S(1)} %pad_maximum_fusion.weight, f32[1,4096]{1,0:T(1,128)S(1)} %bitcast.53, f32[1,256]{1,0:T(1,128)S(1)} %bitcast.57, bf16[4,64,1024]{2,1,0:T(8,128)(2,1)S(1)} %pad_maximum_fusion.7.refs_0_, ...), custom_call_target="tpu_custom_call" | custom-call | flops 536870912 | bytes 4194304 | tf_op jit(solution)/shard_map/pallas_call | solution.py:101
  169.7 5.8 %collective-permute-start.39 = (f32[256,256]{1,0:T(8,128)S(1)}, f32[256,256]{1,0:T(8,128)S(1)}, u32[]{:S(2)}, u32[]{:S(2)}) collective-permute-start(f32[256,256]{1,0:T(8,128)S(1)} %get-tuple-element.47.own), channel_id=1, source_target_pairs={{0,1},{1,0},{2,3},{3,2},{4,5},{5,4},{6,7},{7,6},{8,9},{9,8},{10,11... | collective-permute-start | bytes 786440 | tf_op jit(solution)/shard_map/ppermute | solution.py:43
  176.7 1.9 %shard_map.93 = (f32[128,4096]{1,0:T(8,128)S(1)}, bf16[128,4096]{1,0:T(8,128)(2,1)S(1)}) custom-call(f32[256,256]{1,0:T(8,128)S(1)} %get-tuple-element.47.own, f32[256,256]{1,0:T(8,128)S(1)} %collective-permute-done.39.other, f32[256,256]{1,0:T(8,128)S(1)} %get-tuple-element.48.preact, bf16[256,256]{1,0:T(8,128)(2,1)S(1)} %get-tuple-element.49.flat, ...), custom_call_target="tpu_custom_call" | custom-call | flops 1073741824 | bytes 12582912 | tf_op jit(solution)/shard_map/pallas_call | solution.py:211
  179.1 3.4 %shard_map.94 = (bf16[128,8192]{1,0:T(8,128)(2,1)}, bf16[128,8192]{1,0:T(8,128)(2,1)}, bf16[128,8192]{1,0:T(8,128)(2,1)}) custom-call(s32[1]{0:T(128)} %bitcast.at, f32[128,4096]{1,0:T(8,128)S(1)} %get-tuple-element.53.gradient_ref, bf16[128,8192]{1,0:T(8,128)(2,1)S(1)} %copy-done, bf16[128,8192]{1,0:T(8,128)(2,1)S(1)} %copy-done.1), custom_call_target="tpu_custom_call" | custom-call | flops 10485760 | bytes 7340032 | tf_op jit(solution)/shard_map/pallas_call | solution.py:239
  182.5 3.4 %shard_map.95 = (bf16[128,8192]{1,0:T(8,128)(2,1)}, bf16[128,8192]{1,0:T(8,128)(2,1)}, bf16[128,8192]{1,0:T(8,128)(2,1)}) custom-call(s32[1]{0:T(128)S(6)} %sub.15.at, bf16[128,4096]{1,0:T(8,128)(2,1)S(1)} %collective-permute-done.40.gradient_ref, bf16[128,8192]{1,0:T(8,128)(2,1)S(1)} %copy-done, ...), custom_call_target="tpu_custom_call", output_to_operand_aliasing={{0}: (4, {}), {1}: (5, {}), {2}: (6, {})} | custom-call | flops 10485760 | bytes 7340032 | tf_op jit(solution)/shard_map/pallas_call | solution.py:239
  (96 shorter events, 19.5 us)
Async XLA Ops:
  1.4 4.1 %collective-permute-start.1 = (bf16[16,1024]{1,0:T(8,128)(2,1)S(1)}, bf16[16,1024]{1,0:T(8,128)(2,1)S(1)}, u32[]{:S(2)}, u32[]{:S(2)}) collective-permute-start(bf16[16,1024]{1,0:T(8,128)(2,1)S(1)} %constant_dynamic-slice_fusion), channel_id=1, source_target_pairs={{0,1},{1,0},{2,3},{3,2},{4,5},{5,4},{6,7},{7,6},{8,9},{9,8},{10,11... | collective-permute-start | bytes 98312 | tf_op jit(solution)/shard_map/ppermute | solution.py:43
  6.3 9.5 %collective-permute-start.2 = (bf16[32,1024]{1,0:T(8,128)(2,1)S(1)}, bf16[32,1024]{1,0:T(8,128)(2,1)S(1)}, u32[]{:S(2)}, u32[]{:S(2)}) collective-permute-start(bf16[32,1024]{1,0:T(8,128)(2,1)S(1)} %get-tuple-element.86), channel_id=1, source_target_pairs={{0,4},{2,6},{4,0},{6,2},{1,5},{3,7},{5,1},{7,3},{8,12},{10,14},{12... | collective-permute-start | bytes 196616 | tf_op jit(solution)/shard_map/ppermute | solution.py:269
  11.6 35.8 %collective-permute-start = (bf16[128,8192]{1,0:T(8,128)(2,1)}, bf16[128,8192]{1,0:T(8,128)(2,1)}, u32[]{:S(2)}, u32[]{:S(2)}) collective-permute-start(bf16[128,8192]{1,0:T(8,128)(2,1)} %param.8), channel_id=1, source_target_pairs={{0,1},{1,0},{2,3},{3,2},{4,5},{5,4},{6,7},{7,6},{8,9},{9,8},{10,11... | collective-permute-start | bytes 6291464 | tf_op jit(solution)/shard_map/ppermute | solution.py:43
  12.2 6.6 %collective-permute-start.3 = (bf16[32,1024]{1,0:T(8,128)(2,1)S(1)}, bf16[32,1024]{1,0:T(8,128)(2,1)S(1)}, u32[]{:S(2)}, u32[]{:S(2)}) collective-permute-start(bf16[32,1024]{1,0:T(8,128)(2,1)S(1)} %get-tuple-element.86), channel_id=1, source_target_pairs={{0,2},{2,4},{4,6},{6,0},{1,3},{3,5},{5,7},{7,1},{8,10},{10,12},{12... | collective-permute-start | bytes 196616 | tf_op jit(solution)/shard_map/ppermute | solution.py:269
  13.4 5.4 %collective-permute-start.4 = (bf16[32,1024]{1,0:T(8,128)(2,1)S(1)}, bf16[32,1024]{1,0:T(8,128)(2,1)S(1)}, u32[]{:S(2)}, u32[]{:S(2)}) collective-permute-start(bf16[32,1024]{1,0:T(8,128)(2,1)S(1)} %get-tuple-element.86), channel_id=1, source_target_pairs={{0,6},{2,0},{4,2},{6,4},{1,7},{3,1},{5,3},{7,5},{8,14},{10,8},{12,... | collective-permute-start | bytes 196616 | tf_op jit(solution)/shard_map/ppermute | solution.py:269
  18.9 7.1 %collective-permute-start.5 = (bf16[128,1024]{1,0:T(8,128)(2,1)S(1)}, bf16[128,1024]{1,0:T(8,128)(2,1)S(1)}, u32[]{:S(2)}, u32[]{:S(2)}) collective-permute-start(bf16[128,1024]{1,0:T(8,128)(2,1)S(1)} %constant_dynamic-update-slice_fusion.source), channel_id=1, source_target_pairs={{0,16},{1,129},{8,24},{9,137},{16,0},{17,145},{24,8},{25,153},{64,... | collective-permute-start | bytes 786440 | tf_op jit(solution)/shard_map/ppermute | solution.py:39
  21.7 13.1 %copy-start.2 = (f32[8192]{0:T(1024)S(1)}, f32[8192]{0:T(1024)}, u32[]{:S(2)}) copy-start(f32[8192]{0:T(1024)} %param.7) | copy-start | bytes 98308
  21.7 13.1 %copy-start.3 = (f32[128]{0:T(128)S(1)}, f32[128]{0:T(128)}, u32[]{:S(2)}) copy-start(f32[128]{0:T(128)} %param.9) | copy-start | bytes 1540
  21.7 7.1 %collective-permute-start.6 = (bf16[128,1024]{1,0:T(8,128)(2,1)S(1)}, bf16[128,1024]{1,0:T(8,128)(2,1)S(1)}, u32[]{:S(2)}, u32[]{:S(2)}) collective-permute-start(bf16[128,1024]{1,0:T(8,128)(2,1)S(1)} %constant_dynamic-update-slice_fusion.source), channel_id=1, source_target_pairs={{0,8},{1,65},{8,16},{9,73},{16,24},{17,81},{24,0},{25,89},{64,72},... | collective-permute-start | bytes 786440 | tf_op jit(solution)/shard_map/ppermute | solution.py:39
  22.0 6.9 %collective-permute-start.7 = (bf16[128,1024]{1,0:T(8,128)(2,1)S(1)}, bf16[128,1024]{1,0:T(8,128)(2,1)S(1)}, u32[]{:S(2)}, u32[]{:S(2)}) collective-permute-start(bf16[128,1024]{1,0:T(8,128)(2,1)S(1)} %constant_dynamic-update-slice_fusion.source), channel_id=1, source_target_pairs={{0,24},{1,193},{8,0},{9,201},{16,8},{17,209},{24,16},{25,217},{64,... | collective-permute-start | bytes 786440 | tf_op jit(solution)/shard_map/ppermute | solution.py:39
  29.0 9.7 %collective-permute-start.17 = (bf16[4,64,1024]{2,1,0:T(8,128)(2,1)S(1)}, bf16[4,64,1024]{2,1,0:T(8,128)(2,1)S(1)}, u32[]{:S(2)}, u32[]{:S(2)}) collective-permute-start(bf16[4,64,1024]{2,1,0:T(8,128)(2,1)S(1)} %pad_maximum_fusion.4.refs_0_), channel_id=1, source_target_pairs={{0,64},{1,9},{8,72},{9,17},{16,80},{17,25},{24,88},{25,1},{64,128}... | collective-permute-start | bytes 1572872 | tf_op jit(solution)/shard_map/ppermute | solution.py:39
  30.4 8.4 %collective-permute-start.18 = (bf16[4,64,1024]{2,1,0:T(8,128)(2,1)S(1)}, bf16[4,64,1024]{2,1,0:T(8,128)(2,1)S(1)}, u32[]{:S(2)}, u32[]{:S(2)}) collective-permute-start(bf16[4,64,1024]{2,1,0:T(8,128)(2,1)S(1)} %pad_maximum_fusion.4.refs_0_), channel_id=1, source_target_pairs={{0,192},{1,25},{8,200},{9,1},{16,208},{17,9},{24,216},{25,17},{64,... | collective-permute-start | bytes 1572872 | tf_op jit(solution)/shard_map/ppermute | solution.py:39
  32.0 12.3 %collective-permute-start.8 = (bf16[4,64,1024]{2,1,0:T(8,128)(2,1)S(1)}, bf16[4,64,1024]{2,1,0:T(8,128)(2,1)S(1)}, u32[]{:S(2)}, u32[]{:S(2)}) collective-permute-start(bf16[4,64,1024]{2,1,0:T(8,128)(2,1)S(1)} %pad_maximum_fusion.1.refs_0_), channel_id=1, source_target_pairs={{0,64},{1,9},{8,72},{9,17},{16,80},{17,25},{24,88},{25,1},{64,128}... | collective-permute-start | bytes 1572872 | tf_op jit(solution)/shard_map/ppermute | solution.py:39
  32.1 12.4 %collective-permute-start.9 = (bf16[4,64,1024]{2,1,0:T(8,128)(2,1)S(1)}, bf16[4,64,1024]{2,1,0:T(8,128)(2,1)S(1)}, u32[]{:S(2)}, u32[]{:S(2)}) collective-permute-start(bf16[4,64,1024]{2,1,0:T(8,128)(2,1)S(1)} %pad_maximum_fusion.1.refs_0_), channel_id=1, source_target_pairs={{0,192},{1,25},{8,200},{9,1},{16,208},{17,9},{24,216},{25,17},{64,... | collective-permute-start | bytes 1572872 | tf_op jit(solution)/shard_map/ppermute | solution.py:39
  38.7 10.2 %collective-permute-start.19 = (bf16[2,64,1024]{2,1,0:T(8,128)(2,1)S(1)}, bf16[2,64,1024]{2,1,0:T(8,128)(2,1)S(1)}, u32[]{:S(2)}, u32[]{:S(2)}) collective-permute-start(bf16[2,64,1024]{2,1,0:T(8,128)(2,1)S(1)} %slice.140), channel_id=1, source_target_pairs={{0,64},{1,9},{8,72},{9,17},{16,80},{17,25},{24,88},{25,1},{64,128}... | collective-permute-start | bytes 786440 | tf_op jit(solution)/shard_map/ppermute | solution.py:39
  38.8 10.1 %collective-permute-start.20 = (bf16[2,64,1024]{2,1,0:T(8,128)(2,1)S(1)}, bf16[2,64,1024]{2,1,0:T(8,128)(2,1)S(1)}, u32[]{:S(2)}, u32[]{:S(2)}) collective-permute-start(bf16[2,64,1024]{2,1,0:T(8,128)(2,1)S(1)} %slice.141), channel_id=1, source_target_pairs={{0,192},{1,25},{8,200},{9,1},{16,208},{17,9},{24,216},{25,17},{64,... | collective-permute-start | bytes 786440 | tf_op jit(solution)/shard_map/ppermute | solution.py:39
  44.3 11.1 %collective-permute-start.10 = (bf16[2,64,1024]{2,1,0:T(8,128)(2,1)S(1)}, bf16[2,64,1024]{2,1,0:T(8,128)(2,1)S(1)}, u32[]{:S(2)}, u32[]{:S(2)}) collective-permute-start(bf16[2,64,1024]{2,1,0:T(8,128)(2,1)S(1)} %slice.134), channel_id=1, source_target_pairs={{0,64},{1,9},{8,72},{9,17},{16,80},{17,25},{24,88},{25,1},{64,128}... | collective-permute-start | bytes 786440 | tf_op jit(solution)/shard_map/ppermute | solution.py:39
  44.4 11.0 %collective-permute-start.11 = (bf16[2,64,1024]{2,1,0:T(8,128)(2,1)S(1)}, bf16[2,64,1024]{2,1,0:T(8,128)(2,1)S(1)}, u32[]{:S(2)}, u32[]{:S(2)}) collective-permute-start(bf16[2,64,1024]{2,1,0:T(8,128)(2,1)S(1)} %slice.135), channel_id=1, source_target_pairs={{0,192},{1,25},{8,200},{9,1},{16,208},{17,9},{24,216},{25,17},{64,... | collective-permute-start | bytes 786440 | tf_op jit(solution)/shard_map/ppermute | solution.py:39
  51.4 6.6 %collective-permute-start.21 = (f32[256,256]{1,0:T(8,128)S(1)}, f32[256,256]{1,0:T(8,128)S(1)}, u32[]{:S(2)}, u32[]{:S(2)}) collective-permute-start(f32[256,256]{1,0:T(8,128)S(1)} %get-tuple-element.36.own), channel_id=1, source_target_pairs={{0,1},{1,0},{2,3},{3,2},{4,5},{5,4},{6,7},{7,6},{8,9},{9,8},{10,11... | collective-permute-start | bytes 786440 | tf_op jit(solution)/shard_map/ppermute | solution.py:43
  58.0 5.3 %collective-permute-start.12 = (f32[256,256]{1,0:T(8,128)S(1)}, f32[256,256]{1,0:T(8,128)S(1)}, u32[]{:S(2)}, u32[]{:S(2)}) collective-permute-start(f32[256,256]{1,0:T(8,128)S(1)} %get-tuple-element.30.own), channel_id=1, source_target_pairs={{0,1},{1,0},{2,3},{3,2},{4,5},{5,4},{6,7},{7,6},{8,9},{9,8},{10,11... | collective-permute-start | bytes 786440 | tf_op jit(solution)/shard_map/ppermute | solution.py:43
  60.4 8.0 %collective-permute-start.22 = (bf16[2,64,1024]{2,1,0:T(8,128)(2,1)S(1)}, bf16[2,64,1024]{2,1,0:T(8,128)(2,1)S(1)}, u32[]{:S(2)}, u32[]{:S(2)}) collective-permute-start(bf16[2,64,1024]{2,1,0:T(8,128)(2,1)S(1)} %get-tuple-element.39), channel_id=1, source_target_pairs={{0,64},{1,9},{8,72},{9,17},{16,80},{17,25},{24,88},{25,1},{64,128}... | collective-permute-start | bytes 786440 | tf_op jit(solution)/shard_map/ppermute | solution.py:39
  61.6 6.9 %collective-permute-start.24 = (bf16[2,64,1024]{2,1,0:T(8,128)(2,1)S(1)}, bf16[2,64,1024]{2,1,0:T(8,128)(2,1)S(1)}, u32[]{:S(2)}, u32[]{:S(2)}) collective-permute-start(bf16[2,64,1024]{2,1,0:T(8,128)(2,1)S(1)} %get-tuple-element.41), channel_id=1, source_target_pairs={{0,192},{1,25},{8,200},{9,1},{16,208},{17,9},{24,216},{25,17},{64,... | collective-permute-start | bytes 786440 | tf_op jit(solution)/shard_map/ppermute | solution.py:39
  65.6 6.8 %collective-permute-start.13 = (bf16[2,64,1024]{2,1,0:T(8,128)(2,1)S(1)}, bf16[2,64,1024]{2,1,0:T(8,128)(2,1)S(1)}, u32[]{:S(2)}, u32[]{:S(2)}) collective-permute-start(bf16[2,64,1024]{2,1,0:T(8,128)(2,1)S(1)} %get-tuple-element.33), channel_id=1, source_target_pairs={{0,64},{1,9},{8,72},{9,17},{16,80},{17,25},{24,88},{25,1},{64,128}... | collective-permute-start | bytes 786440 | tf_op jit(solution)/shard_map/ppermute | solution.py:39
  65.7 6.9 %collective-permute-start.15 = (bf16[2,64,1024]{2,1,0:T(8,128)(2,1)S(1)}, bf16[2,64,1024]{2,1,0:T(8,128)(2,1)S(1)}, u32[]{:S(2)}, u32[]{:S(2)}) collective-permute-start(bf16[2,64,1024]{2,1,0:T(8,128)(2,1)S(1)} %get-tuple-element.35), channel_id=1, source_target_pairs={{0,192},{1,25},{8,200},{9,1},{16,208},{17,9},{24,216},{25,17},{64,... | collective-permute-start | bytes 786440 | tf_op jit(solution)/shard_map/ppermute | solution.py:39
  68.5 9.6 %collective-permute-start.23 = (bf16[4,64,1024]{2,1,0:T(8,128)(2,1)S(1)}, bf16[4,64,1024]{2,1,0:T(8,128)(2,1)S(1)}, u32[]{:S(2)}, u32[]{:S(2)}) collective-permute-start(bf16[4,64,1024]{2,1,0:T(8,128)(2,1)S(1)} %pad_maximum_fusion.5), channel_id=1, source_target_pairs={{0,64},{1,9},{8,72},{9,17},{16,80},{17,25},{24,88},{25,1},{64,128}... | collective-permute-start | bytes 1572872 | tf_op jit(solution)/shard_map/ppermute | solution.py:39
  68.7 9.4 %collective-permute-start.25 = (bf16[4,64,1024]{2,1,0:T(8,128)(2,1)S(1)}, bf16[4,64,1024]{2,1,0:T(8,128)(2,1)S(1)}, u32[]{:S(2)}, u32[]{:S(2)}) collective-permute-start(bf16[4,64,1024]{2,1,0:T(8,128)(2,1)S(1)} %pad_maximum_fusion.6), channel_id=1, source_target_pairs={{0,192},{1,25},{8,200},{9,1},{16,208},{17,9},{24,216},{25,17},{64,... | collective-permute-start | bytes 1572872 | tf_op jit(solution)/shard_map/ppermute | solution.py:39
  72.5 11.2 %collective-permute-start.14 = (bf16[4,64,1024]{2,1,0:T(8,128)(2,1)S(1)}, bf16[4,64,1024]{2,1,0:T(8,128)(2,1)S(1)}, u32[]{:S(2)}, u32[]{:S(2)}) collective-permute-start(bf16[4,64,1024]{2,1,0:T(8,128)(2,1)S(1)} %pad_maximum_fusion.2), channel_id=1, source_target_pairs={{0,64},{1,9},{8,72},{9,17},{16,80},{17,25},{24,88},{25,1},{64,128}... | collective-permute-start | bytes 1572872 | tf_op jit(solution)/shard_map/ppermute | solution.py:39
  72.7 11.0 %collective-permute-start.16 = (bf16[4,64,1024]{2,1,0:T(8,128)(2,1)S(1)}, bf16[4,64,1024]{2,1,0:T(8,128)(2,1)S(1)}, u32[]{:S(2)}, u32[]{:S(2)}) collective-permute-start(bf16[4,64,1024]{2,1,0:T(8,128)(2,1)S(1)} %pad_maximum_fusion.3), channel_id=1, source_target_pairs={{0,192},{1,25},{8,200},{9,1},{16,208},{17,9},{24,216},{25,17},{64,... | collective-permute-start | bytes 1572872 | tf_op jit(solution)/shard_map/ppermute | solution.py:39
  84.1 7.1 %collective-permute-start.26 = (bf16[128,1024]{1,0:T(8,128)(2,1)S(1)}, bf16[128,1024]{1,0:T(8,128)(2,1)S(1)}, u32[]{:S(2)}, u32[]{:S(2)}) collective-permute-start(bf16[128,1024]{1,0:T(8,128)(2,1)S(1)} %get-tuple-element.57), channel_id=1, source_target_pairs={{0,16},{1,129},{8,24},{9,137},{16,0},{17,145},{24,8},{25,153},{64,... | collective-permute-start | bytes 786440 | tf_op jit(solution)/shard_map/ppermute | solution.py:39
  85.5 8.5 %collective-permute-start.27 = (bf16[128,1024]{1,0:T(8,128)(2,1)S(1)}, bf16[128,1024]{1,0:T(8,128)(2,1)S(1)}, u32[]{:S(2)}, u32[]{:S(2)}) collective-permute-start(bf16[128,1024]{1,0:T(8,128)(2,1)S(1)} %get-tuple-element.59), channel_id=1, source_target_pairs={{0,8},{1,65},{8,16},{9,73},{16,24},{17,81},{24,0},{25,89},{64,72},... | collective-permute-start | bytes 786440 | tf_op jit(solution)/shard_map/ppermute | solution.py:39
  87.8 6.9 %collective-permute-start.28 = (bf16[128,1024]{1,0:T(8,128)(2,1)S(1)}, bf16[128,1024]{1,0:T(8,128)(2,1)S(1)}, u32[]{:S(2)}, u32[]{:S(2)}) collective-permute-start(bf16[128,1024]{1,0:T(8,128)(2,1)S(1)} %get-tuple-element.58), channel_id=1, source_target_pairs={{0,24},{1,193},{8,0},{9,201},{16,8},{17,209},{24,16},{25,217},{64,... | collective-permute-start | bytes 786440 | tf_op jit(solution)/shard_map/ppermute | solution.py:39
  121.2 6.8 %collective-permute-start.29 = (bf16[128,1024]{1,0:T(8,128)(2,1)S(1)}, bf16[128,1024]{1,0:T(8,128)(2,1)S(1)}, u32[]{:S(2)}, u32[]{:S(2)}) collective-permute-start(bf16[128,1024]{1,0:T(8,128)(2,1)S(1)} %bitcast.58), channel_id=1, source_target_pairs={{0,16},{1,129},{8,24},{9,137},{16,0},{17,145},{24,8},{25,153},{64,... | collective-permute-start | bytes 786440 | tf_op jit(solution)/shard_map/ppermute | solution.py:39
  122.0 8.7 %collective-permute-start.30 = (bf16[128,1024]{1,0:T(8,128)(2,1)S(1)}, bf16[128,1024]{1,0:T(8,128)(2,1)S(1)}, u32[]{:S(2)}, u32[]{:S(2)}) collective-permute-start(bf16[128,1024]{1,0:T(8,128)(2,1)S(1)} %bitcast.59), channel_id=1, source_target_pairs={{0,8},{1,65},{8,16},{9,73},{16,24},{17,81},{24,0},{25,89},{64,72},... | collective-permute-start | bytes 786440 | tf_op jit(solution)/shard_map/ppermute | solution.py:39
  124.3 6.9 %collective-permute-start.31 = (bf16[128,1024]{1,0:T(8,128)(2,1)S(1)}, bf16[128,1024]{1,0:T(8,128)(2,1)S(1)}, u32[]{:S(2)}, u32[]{:S(2)}) collective-permute-start(bf16[128,1024]{1,0:T(8,128)(2,1)S(1)} %bitcast.60), channel_id=1, source_target_pairs={{0,24},{1,193},{8,0},{9,201},{16,8},{17,209},{24,16},{25,217},{64,... | collective-permute-start | bytes 786440 | tf_op jit(solution)/shard_map/ppermute | solution.py:39
  131.3 10.8 %collective-permute-start.35 = (bf16[4,64,1024]{2,1,0:T(8,128)(2,1)S(1)}, bf16[4,64,1024]{2,1,0:T(8,128)(2,1)S(1)}, u32[]{:S(2)}, u32[]{:S(2)}) collective-permute-start(bf16[4,64,1024]{2,1,0:T(8,128)(2,1)S(1)} %pad_maximum_fusion.8.refs_0_), channel_id=1, source_target_pairs={{0,128},{1,17},{8,136},{9,25},{16,144},{17,1},{24,152},{25,9},{64,... | collective-permute-start | bytes 1572872 | tf_op jit(solution)/shard_map/ppermute | solution.py:39
  132.4 15.3 %collective-permute-start.36 = (bf16[4,64,1024]{2,1,0:T(8,128)(2,1)S(1)}, bf16[4,64,1024]{2,1,0:T(8,128)(2,1)S(1)}, u32[]{:S(2)}, u32[]{:S(2)}) collective-permute-start(bf16[4,64,1024]{2,1,0:T(8,128)(2,1)S(1)} %pad_maximum_fusion.8.refs_0_), channel_id=1, source_target_pairs={{0,64},{1,9},{8,72},{9,17},{16,80},{17,25},{24,88},{25,1},{64,128}... | collective-permute-start | bytes 1572872 | tf_op jit(solution)/shard_map/ppermute | solution.py:39
  134.9 12.8 %collective-permute-start.37 = (bf16[4,64,1024]{2,1,0:T(8,128)(2,1)S(1)}, bf16[4,64,1024]{2,1,0:T(8,128)(2,1)S(1)}, u32[]{:S(2)}, u32[]{:S(2)}) collective-permute-start(bf16[4,64,1024]{2,1,0:T(8,128)(2,1)S(1)} %pad_maximum_fusion.8.refs_0_), channel_id=1, source_target_pairs={{0,192},{1,25},{8,200},{9,1},{16,208},{17,9},{24,216},{25,17},{64,... | collective-permute-start | bytes 1572872 | tf_op jit(solution)/shard_map/ppermute | solution.py:39
  135.1 32.2 %collective-permute-start.32 = (bf16[4,64,1024]{2,1,0:T(8,128)(2,1)S(1)}, bf16[4,64,1024]{2,1,0:T(8,128)(2,1)S(1)}, u32[]{:S(2)}, u32[]{:S(2)}) collective-permute-start(bf16[4,64,1024]{2,1,0:T(8,128)(2,1)S(1)} %pad_maximum_fusion.7.refs_0_), channel_id=1, source_target_pairs={{0,128},{1,17},{8,136},{9,25},{16,144},{17,1},{24,152},{25,9},{64,... | collective-permute-start | bytes 1572872 | tf_op jit(solution)/shard_map/ppermute | solution.py:39
  136.9 30.5 %collective-permute-start.33 = (bf16[4,64,1024]{2,1,0:T(8,128)(2,1)S(1)}, bf16[4,64,1024]{2,1,0:T(8,128)(2,1)S(1)}, u32[]{:S(2)}, u32[]{:S(2)}) collective-permute-start(bf16[4,64,1024]{2,1,0:T(8,128)(2,1)S(1)} %pad_maximum_fusion.7.refs_0_), channel_id=1, source_target_pairs={{0,64},{1,9},{8,72},{9,17},{16,80},{17,25},{24,88},{25,1},{64,128}... | collective-permute-start | bytes 1572872 | tf_op jit(solution)/shard_map/ppermute | solution.py:39
  142.2 25.2 %collective-permute-start.34 = (bf16[4,64,1024]{2,1,0:T(8,128)(2,1)S(1)}, bf16[4,64,1024]{2,1,0:T(8,128)(2,1)S(1)}, u32[]{:S(2)}, u32[]{:S(2)}) collective-permute-start(bf16[4,64,1024]{2,1,0:T(8,128)(2,1)S(1)} %pad_maximum_fusion.7.refs_0_), channel_id=1, source_target_pairs={{0,192},{1,25},{8,200},{9,1},{16,208},{17,9},{24,216},{25,17},{64,... | collective-permute-start | bytes 1572872 | tf_op jit(solution)/shard_map/ppermute | solution.py:39
  150.1 15.4 %collective-permute-start.38 = (f32[256,256]{1,0:T(8,128)S(1)}, f32[256,256]{1,0:T(8,128)S(1)}, u32[]{:S(2)}, u32[]{:S(2)}) collective-permute-start(f32[256,256]{1,0:T(8,128)S(1)} %get-tuple-element.42.own), channel_id=1, source_target_pairs={{0,1},{1,0},{2,3},{3,2},{4,5},{5,4},{6,7},{7,6},{8,9},{9,8},{10,11... | collective-permute-start | bytes 786440 | tf_op jit(solution)/shard_map/ppermute | solution.py:43
  169.7 7.0 %collective-permute-start.39 = (f32[256,256]{1,0:T(8,128)S(1)}, f32[256,256]{1,0:T(8,128)S(1)}, u32[]{:S(2)}, u32[]{:S(2)}) collective-permute-start(f32[256,256]{1,0:T(8,128)S(1)} %get-tuple-element.47.own), channel_id=1, source_target_pairs={{0,1},{1,0},{2,3},{3,2},{4,5},{5,4},{6,7},{7,6},{8,9},{9,8},{10,11... | collective-permute-start | bytes 786440 | tf_op jit(solution)/shard_map/ppermute | solution.py:43
  176.7 2.3 %copy-start = (bf16[128,8192]{1,0:T(8,128)(2,1)S(1)}, bf16[128,8192]{1,0:T(8,128)(2,1)}, u32[]{:S(2)}) copy-start(bf16[128,8192]{1,0:T(8,128)(2,1)} %first_ref.3) | copy-start | bytes 6291460
  176.7 2.3 %copy-start.1 = (bf16[128,8192]{1,0:T(8,128)(2,1)S(1)}, bf16[128,8192]{1,0:T(8,128)(2,1)}, u32[]{:S(2)}) copy-start(bf16[128,8192]{1,0:T(8,128)(2,1)} %second_ref.3) | copy-start | bytes 6291460
  178.6 3.9 %collective-permute-start.40 = (bf16[128,4096]{1,0:T(8,128)(2,1)S(1)}, bf16[128,4096]{1,0:T(8,128)(2,1)S(1)}, u32[]{:S(2)}, u32[]{:S(2)}) collective-permute-start(bf16[128,4096]{1,0:T(8,128)(2,1)S(1)} %get-tuple-element.52), channel_id=1, source_target_pairs={{0,1},{1,0},{2,3},{3,2},{4,5},{5,4},{6,7},{7,6},{8,9},{9,8},{10,11... | collective-permute-start | bytes 3145736 | tf_op jit(solution)/shard_map/ppermute | solution.py:43
where the time goes:
time: 186 us
  starting transfers between devices  81 us (44%)
  waiting for transfers between devices  46.4 us (25%)
  blocking collectives  25.7 us (14%)
  Pallas kernels  25.6 us (14%)
  local copies, waits for them, and re-layouts  3.64 us (2%)
  other arithmetic  2.49 us (1%)
    ppermute x31, starting transfers between devices, shift(): return lax.ppermute(value, PLANE, plane_pairs(by, last))  43.7 us
    ppermute x31, waiting for transfers between devices, shift(): return lax.ppermute(value, PLANE, plane_pairs(by, last))  40.2 us
    ppermute x7, starting transfers between devices, swap(): return lax.ppermute(value, 'c', [(0, 1), (1, 0)])  28.5 us
    all_to_all x1, blocking collectives, body(): lax.all_to_all(strip.astype(BF16).reshape(8, thin, part), Z, 0, 0, tiled=...  14 us
    all_to_all x1, blocking collectives, body(): error = lax.all_to_all(error, Z, 0, 0, tiled=True)  11.7 us
    pallas_call x4, Pallas kernels, project(): pl.pallas_call(functools.partial(project_kernel, centre=centre), out_shap...  9.72 us
    ppermute x3, starting transfers between devices, body(): lax.ppermute(both, 'zh', [(i, (i + by) % SIDE) for i in range(SIDE)])  8.84 us
    pallas_call x2, Pallas kernels, adam(): pl.pallas_call(functools.partial(adam_kernel, rows=rows), out_shape=(jax....  6.85 us
  transfers between devices with their start and end apart: 41, of which 20 were waited for; matrix products, arithmetic and copies ran while one was open for 2% of the time, Pallas kernels for 9%

commit v1 on v0

--- a/solution.py
+++ b/solution.py
@@ -67,7 +67,7 @@
     return pl.multiple_of(row * thick, thick), pl.multiple_of(column * part, part)
 
 
-def project_kernel(me, weight, extra, lift, *refs, centre):
+def project_kernel(me, weight, extra, lift, *refs, centre, looped):
     layout = LAYOUT if centre else WHOLE
     pieces, (laid, product) = refs[: len(layout)], refs[-2:]
     thick, part = pieces[0].shape[1:]
@@ -82,24 +82,32 @@
             return carry
 
         lax.fori_loop(0, len(blocks), place, 0)
-    product[...] = jnp.broadcast_to(lift[...], product.shape) if centre else jnp.zeros_like(product)
-
-    def multiply(q, carry):
-        columns = pl.ds(pl.multiple_of(q * part, part), part)
-        product[...] += lax.dot_general(
+
+    def term(columns):
+        return lax.dot_general(
             laid[:, columns], weight[:, columns], (((1,), (1,)), ((), ())), preferred_element_type=F32
         )
+
+    def add(q, carry):
+        product[...] += term(pl.ds(pl.multiple_of(q * part, part), part))
         return carry
 
-    lax.fori_loop(0, SIDE, multiply, 0)
-
-
-def project(me, weight, extra, lift, pieces, centre, after=()):
+    if looped:
+        product[...] = term(pl.ds(0, part))
+        lax.fori_loop(1, SIDE, add, 0)
+    else:
+        total = lift[...] if centre else None
+        for q in range(SIDE):
+            total = term(pl.ds(q * part, part)) if total is None else total + term(pl.ds(q * part, part))
+        product[...] = total
+
+
+def project(me, weight, extra, lift, pieces, centre, after=(), looped=False):
     thick, part = pieces[0].shape[1:]
     rows, width = thick * SIDE, part * SIDE
     args = (me, weight, extra, lift, *pieces, *after)
     return pl.pallas_call(
-        functools.partial(project_kernel, centre=centre),
+        functools.partial(project_kernel, centre=centre, looped=looped),
         out_shape=(jax.ShapeDtypeStruct((rows, width), BF16), jax.ShapeDtypeStruct((rows, weight.shape[0]), F32)),
         in_specs=[SMEM] + [VMEM] * (3 + len(pieces)) + [pl.BlockSpec(memory_space=pl.ANY)] * len(after),
         out_specs=(VMEM, VMEM),
@@ -114,7 +122,7 @@
     return jnp.concatenate([own[:, :latents] + other[:, latents:], own[:, latents:] + other[:, :latents]], 1)
 
 
-def recon_kernel(me, own, other, weight, preact, flat, *refs):
+def recon_kernel(me, own, other, weight, preact, flat, *refs, looped):
     blocks, (activity, laid) = refs[:PIECES], refs[PIECES:]
     _, thick, part = blocks[0].shape
     value = join(own[...], other[...], own.shape[1] // 2)
@@ -128,7 +136,7 @@
         laid[:, columns] = jnp.dot(activity[...], weight[:, columns], preferred_element_type=F32).astype(BF16)
         return carry
 
-    lax.fori_loop(0, SIDE, multiply, 0)
+    lax.fori_loop(0, SIDE, multiply, 0, unroll=not looped)
     for piece, (away, wanted) in zip(blocks, LAYOUT):
 
         def take(i, carry, piece=piece, away=away, begin=wanted[0]):
@@ -139,7 +147,7 @@
         lax.fori_loop(0, len(wanted), take, 0)
 
 
-def recon(me, own, other, weight):
+def recon(me, own, other, weight, looped):
     rows, wide = own.shape
     width = weight.shape[1]
     args = (me, own, other, weight)
@@ -147,7 +155,7 @@
     for _, wanted in LAYOUT:
         shapes.append(jax.ShapeDtypeStruct((len(wanted), rows // SIDE, width // SIDE), BF16))
     return pl.pallas_call(
-        recon_kernel,
+        functools.partial(recon_kernel, looped=looped),
         out_shape=tuple(shapes),
         in_specs=[SMEM] + [VMEM] * 3,
         out_specs=(VMEM,) * len(shapes),
@@ -200,7 +208,8 @@
     lax.fori_loop(0, error.shape[1] // chunk, step, 0)
 
 
-def gradient(args, before, chunk=1024):
+def gradient(args, before):
+    chunk = 512 if before is None else 1024
     flat, error = args[3], args[4]
     wide, width = flat.shape[0], error.shape[1]
     if before is None:
@@ -221,13 +230,20 @@
 
 def adam_kernel(at, gradient_ref, first_ref, second_ref, *refs, rows):
     update_out, first_out, second_out = refs[-3:]
-    gradient = gradient_ref[...].astype(F32) * (1.0 / rows)
-    first = 0.9 * first_ref[...].astype(F32) + 0.1 * gradient
-    second = 0.999 * second_ref[...].astype(F32) + 0.001 * gradient * gradient
-    update = first * (1.0 / (1.0 - 0.9**STEP)) / (jnp.sqrt(second * (1.0 / (1.0 - 0.999**STEP))) + 1e-08)
-    update_out[...] = update.astype(BF16)
-    first_out[...] = first.astype(BF16)
-    second_out[...] = second.astype(BF16)
+    strip = 16
+
+    def step(i, carry):
+        here = pl.ds(pl.multiple_of(i * strip, strip), strip)
+        gradient = gradient_ref[here, :].astype(F32) * (1.0 / rows)
+        first = 0.9 * first_ref[here, :].astype(F32) + 0.1 * gradient
+        second = 0.999 * second_ref[here, :].astype(F32) + 0.001 * gradient * gradient
+        update = first * (1.0 / (1.0 - 0.9**STEP)) / (jnp.sqrt(second * (1.0 / (1.0 - 0.999**STEP))) + 1e-08)
+        update_out[here, :] = update.astype(BF16)
+        first_out[here, :] = first.astype(BF16)
+        second_out[here, :] = second.astype(BF16)
+        return carry
+
+    lax.fori_loop(0, gradient_ref.shape[0] // strip, step, 0)
 
 
 def adam(at, gradient, first_moment, second_moment, outs, rows, chunk=1024):
@@ -288,7 +304,7 @@
     ahead, made = [], []
     for k in chunks:
         ahead.append(project(me, pair, decoder, lift, pieces[k], True))
-        made.append(recon(me, ahead[k][1], swap(ahead[k][1]), pair))
+        made.append(recon(me, ahead[k][1], swap(ahead[k][1]), pair, k > 0))
     blocks = jnp.concatenate([fold(*made[k][2:]) for k in chunks], 1)
     strip = blocks[0].astype(F32)
     for by in ORDER[1:]:
@@ -300,7 +316,7 @@
     total = None
     for k in chunks:
         after = () if total is None else (total,)
-        laid, own = project(me, pair, decoder, lift, pieces[k], False, after)
+        laid, own = project(me, pair, decoder, lift, pieces[k], False, after, total is None)
         total = gradient((own, swap(own), made[k][0], made[k][1], laid, ahead[k][0]), total)
     mine, theirs = total
     arrived = swap(theirs)

time: 186 us -> 184 us (0.989)
    pallas_call x6, Pallas kernels: 14.4 us -> 11.8 us  [the longest x4 7.77 us: project(): pl.pallas_call(functools.partial(project_kernel, centre=centre, looped=lo...]
where the time goes in v1:
time: 184 us
  starting transfers between devices  80.6 us (44%)
  waiting for transfers between devices  46.3 us (25%)
  blocking collectives  25.8 us (14%)
  Pallas kernels  23.9 us (13%)
  local copies, waits for them, and re-layouts  3.64 us (2%)
  other arithmetic  2.49 us (1%)
    ppermute x31, starting transfers between devices, shift(): return lax.ppermute(value, PLANE, plane_pairs(by, last))  43.7 us
    ppermute x31, waiting for transfers between devices, shift(): return lax.ppermute(value, PLANE, plane_pairs(by, last))  40 us
    ppermute x7, starting transfers between devices, swap(): return lax.ppermute(value, 'c', [(0, 1), (1, 0)])  28.1 us
    all_to_all x1, blocking collectives, body(): lax.all_to_all(strip.astype(BF16).reshape(8, thin, part), Z, 0, 0, tiled=...  14 us
    all_to_all x1, blocking collectives, body(): error = lax.all_to_all(error, Z, 0, 0, tiled=True)  11.9 us
    ppermute x3, starting transfers between devices, body(): lax.ppermute(both, 'zh', [(i, (i + by) % SIDE) for i in range(SIDE)])  8.84 us
    pallas_call x4, Pallas kernels, project(): pl.pallas_call(functools.partial(project_kernel, centre=centre, looped=lo...  7.77 us
    pallas_call x2, Pallas kernels, adam(): pl.pallas_call(functools.partial(adam_kernel, rows=rows), out_shape=(jax....  7.12 us
  transfers between devices with their start and end apart: 41, of which 20 were waited for; matrix products, arithmetic and copies ran while one was open for 2% of the time, Pallas kernels for 9%

profile of v1, /device:TPU:1, one launch (start us, length us, event | category | flops | bytes accessed | tf_op | source)
XLA Modules:
  0.0 183.8 jit_solution(8688442091586347259)
XLA Ops:
  1.4 3.2 %collective-permute-start.1 = (bf16[16,1024]{1,0:T(8,128)(2,1)S(1)}, bf16[16,1024]{1,0:T(8,128)(2,1)S(1)}, u32[]{:S(2)}, u32[]{:S(2)}) collective-permute-start(bf16[16,1024]{1,0:T(8,128)(2,1)S(1)} %constant_dynamic-slice_fusion), channel_id=1, source_target_pairs={{0,1},{1,0},{2,3},{3,2},{4,5},{5,4},{6,7},{7,6},{8,9},{9,8},{10,11... | collective-permute-start | bytes 98312 | tf_op jit(solution)/shard_map/ppermute | solution.py:43
  6.3 5.3 %collective-permute-start.2 = (bf16[32,1024]{1,0:T(8,128)(2,1)S(1)}, bf16[32,1024]{1,0:T(8,128)(2,1)S(1)}, u32[]{:S(2)}, u32[]{:S(2)}) collective-permute-start(bf16[32,1024]{1,0:T(8,128)(2,1)S(1)} %get-tuple-element.86), channel_id=1, source_target_pairs={{0,4},{2,6},{4,0},{6,2},{1,5},{3,7},{5,1},{7,3},{8,12},{10,14},{12... | collective-permute-start | bytes 196616 | tf_op jit(solution)/shard_map/ppermute | solution.py:285
  13.4 2.4 %collective-permute-start.4 = (bf16[32,1024]{1,0:T(8,128)(2,1)S(1)}, bf16[32,1024]{1,0:T(8,128)(2,1)S(1)}, u32[]{:S(2)}, u32[]{:S(2)}) collective-permute-start(bf16[32,1024]{1,0:T(8,128)(2,1)S(1)} %get-tuple-element.86), channel_id=1, source_target_pairs={{0,6},{2,0},{4,2},{6,4},{1,7},{3,1},{5,3},{7,5},{8,14},{10,8},{12,... | collective-permute-start | bytes 196616 | tf_op jit(solution)/shard_map/ppermute | solution.py:285
  15.8 3.0 %collective-permute-done.3 = bf16[32,1024]{1,0:T(8,128)(2,1)S(1)} collective-permute-done((bf16[32,1024]{1,0:T(8,128)(2,1)S(1)}, bf16[32,1024]{1,0:T(8,128)(2,1)S(1)}, u32[]{:S(2)}, u32[]{:S(2)}) %collective-permute-start.3) | collective-permute-done | bytes 65568 | tf_op jit(solution)/shard_map/ppermute | solution.py:285
  18.9 2.8 %collective-permute-start.5 = (bf16[128,1024]{1,0:T(8,128)(2,1)S(1)}, bf16[128,1024]{1,0:T(8,128)(2,1)S(1)}, u32[]{:S(2)}, u32[]{:S(2)}) collective-permute-start(bf16[128,1024]{1,0:T(8,128)(2,1)S(1)} %constant_dynamic-update-slice_fusion.source), channel_id=1, source_target_pairs={{0,16},{1,129},{8,24},{9,137},{16,0},{17,145},{24,8},{25,153},{64,... | collective-permute-start | bytes 786440 | tf_op jit(solution)/shard_map/ppermute | solution.py:39
  22.0 2.4 %collective-permute-start.7 = (bf16[128,1024]{1,0:T(8,128)(2,1)S(1)}, bf16[128,1024]{1,0:T(8,128)(2,1)S(1)}, u32[]{:S(2)}, u32[]{:S(2)}) collective-permute-start(bf16[128,1024]{1,0:T(8,128)(2,1)S(1)} %constant_dynamic-update-slice_fusion.source), channel_id=1, source_target_pairs={{0,24},{1,193},{8,0},{9,201},{16,8},{17,209},{24,16},{25,217},{64,... | collective-permute-start | bytes 786440 | tf_op jit(solution)/shard_map/ppermute | solution.py:39
  24.4 1.6 collective-permute-done.5
  26.0 2.8 %collective-permute-done.6 = bf16[128,1024]{1,0:T(8,128)(2,1)S(1)} collective-permute-done((bf16[128,1024]{1,0:T(8,128)(2,1)S(1)}, bf16[128,1024]{1,0:T(8,128)(2,1)S(1)}, u32[]{:S(2)}, u32[]{:S(2)}) %collective-permute-start.6) | collective-permute-done | bytes 262176 | tf_op jit(solution)/shard_map/ppermute | solution.py:39
  29.0 1.4 collective-permute-start.17
  30.4 1.5 collective-permute-start.18
  32.1 2.7 %collective-permute-start.9 = (bf16[4,64,1024]{2,1,0:T(8,128)(2,1)S(1)}, bf16[4,64,1024]{2,1,0:T(8,128)(2,1)S(1)}, u32[]{:S(2)}, u32[]{:S(2)}) collective-permute-start(bf16[4,64,1024]{2,1,0:T(8,128)(2,1)S(1)} %pad_maximum_fusion.1.refs_0_), channel_id=1, source_target_pairs={{0,192},{1,25},{8,200},{9,1},{16,208},{17,9},{24,216},{25,17},{64,... | collective-permute-start | bytes 1572872 | tf_op jit(solution)/shard_map/ppermute | solution.py:39
  36.1 2.5 %collective-permute-done.17.refs_1_ = bf16[4,64,1024]{2,1,0:T(8,128)(2,1)S(1)} collective-permute-done((bf16[4,64,1024]{2,1,0:T(8,128)(2,1)S(1)}, bf16[4,64,1024]{2,1,0:T(8,128)(2,1)S(1)}, u32[]{:S(2)}, u32[]{:S(2)}) %collective-permute-start.17) | collective-permute-done | bytes 524320 | tf_op jit(solution)/shard_map/ppermute | solution.py:39
  38.8 2.7 %collective-permute-start.20 = (bf16[2,64,1024]{2,1,0:T(8,128)(2,1)S(1)}, bf16[2,64,1024]{2,1,0:T(8,128)(2,1)S(1)}, u32[]{:S(2)}, u32[]{:S(2)}) collective-permute-start(bf16[2,64,1024]{2,1,0:T(8,128)(2,1)S(1)} %slice.141), channel_id=1, source_target_pairs={{0,192},{1,25},{8,200},{9,1},{16,208},{17,9},{24,216},{25,17},{64,... | collective-permute-start | bytes 786440 | tf_op jit(solution)/shard_map/ppermute | solution.py:39
  41.5 2.7 %collective-permute-done.8.refs_1_ = bf16[4,64,1024]{2,1,0:T(8,128)(2,1)S(1)} collective-permute-done((bf16[4,64,1024]{2,1,0:T(8,128)(2,1)S(1)}, bf16[4,64,1024]{2,1,0:T(8,128)(2,1)S(1)}, u32[]{:S(2)}, u32[]{:S(2)}) %collective-permute-start.8) | collective-permute-done | bytes 524320 | tf_op jit(solution)/shard_map/ppermute | solution.py:39
  44.4 2.9 %collective-permute-start.11 = (bf16[2,64,1024]{2,1,0:T(8,128)(2,1)S(1)}, bf16[2,64,1024]{2,1,0:T(8,128)(2,1)S(1)}, u32[]{:S(2)}, u32[]{:S(2)}) collective-permute-start(bf16[2,64,1024]{2,1,0:T(8,128)(2,1)S(1)} %slice.135), channel_id=1, source_target_pairs={{0,192},{1,25},{8,200},{9,1},{16,208},{17,9},{24,216},{25,17},{64,... | collective-permute-start | bytes 786440 | tf_op jit(solution)/shard_map/ppermute | solution.py:39
  48.9 1.9 %shard_map.87 = (bf16[256,4096]{1,0:T(8,128)(2,1)S(1)}, f32[256,256]{1,0:T(8,128)S(1)}) custom-call(s32[4]{0:T(128)S(1)} %pad_add_fusion.me, bf16[256,4096]{1,0:T(8,128)(2,1)S(1)} %pad_maximum_fusion.weight, f32[1,4096]{1,0:T(1,128)S(1)} %bitcast.49, f32[1,256]{1,0:T(1,128)S(1)} %bitcast.54, bf16[4,64,1024]{2,1,0:T(8,128)(2,1)S(1)} %pad_maximum_fusion.4.refs_0_, ...), custom_call_target="tpu_custom_call" | custom-call | flops 536870912 | bytes 4194304 | tf_op jit(solution)/shard_map/pallas_call | solution.py:109
  50.8 4.0 %collective-permute-start.21 = (f32[256,256]{1,0:T(8,128)S(1)}, f32[256,256]{1,0:T(8,128)S(1)}, u32[]{:S(2)}, u32[]{:S(2)}) collective-permute-start(f32[256,256]{1,0:T(8,128)S(1)} %get-tuple-element.36.own), channel_id=1, source_target_pairs={{0,1},{1,0},{2,3},{3,2},{4,5},{5,4},{6,7},{7,6},{8,9},{9,8},{10,11... | collective-permute-start | bytes 786440 | tf_op jit(solution)/shard_map/ppermute | solution.py:43
  54.8 1.9 %shard_map.85 = (bf16[256,4096]{1,0:T(8,128)(2,1)S(1)}, f32[256,256]{1,0:T(8,128)S(1)}) custom-call(s32[4]{0:T(128)S(1)} %pad_add_fusion.me, bf16[256,4096]{1,0:T(8,128)(2,1)S(1)} %pad_maximum_fusion.weight, f32[1,4096]{1,0:T(1,128)S(1)} %bitcast.50, f32[1,256]{1,0:T(1,128)S(1)} %bitcast.55, bf16[4,64,1024]{2,1,0:T(8,128)(2,1)S(1)} %pad_maximum_fusion.1.refs_0_, ...), custom_call_target="tpu_custom_call" | custom-call | flops 536870912 | bytes 4194304 | tf_op jit(solution)/shard_map/pallas_call | solution.py:109
  57.3 2.3 %shard_map.88 = (f32[256,256]{1,0:T(8,128)S(1)}, bf16[256,256]{1,0:T(8,128)(2,1)S(1)}, bf16[4,64,1024]{2,1,0:T(8,128)(2,1)S(1)}, bf16[4,64,1024]{2,1,0:T(8,128)(...) custom-call(s32[4]{0:T(128)S(1)} %pad_add_fusion.me, ...), custom_call_target="tpu_custom_call" | custom-call | flops 536870912 | bytes 4194304 | tf_op jit(solution)/shard_map/pallas_call | solution.py:157
  60.9 1.7 collective-permute-start.24
  62.5 1.7 shard_map.86
  64.3 2.7 %collective-permute-start.15 = (bf16[2,64,1024]{2,1,0:T(8,128)(2,1)S(1)}, bf16[2,64,1024]{2,1,0:T(8,128)(2,1)S(1)}, u32[]{:S(2)}, u32[]{:S(2)}) collective-permute-start(bf16[2,64,1024]{2,1,0:T(8,128)(2,1)S(1)} %get-tuple-element.35), channel_id=1, source_target_pairs={{0,192},{1,25},{8,200},{9,1},{16,208},{17,9},{24,216},{25,17},{64,... | collective-permute-start | bytes 786440 | tf_op jit(solution)/shard_map/ppermute | solution.py:39
  67.3 2.7 %collective-permute-start.25 = (bf16[4,64,1024]{2,1,0:T(8,128)(2,1)S(1)}, bf16[4,64,1024]{2,1,0:T(8,128)(2,1)S(1)}, u32[]{:S(2)}, u32[]{:S(2)}) collective-permute-start(bf16[4,64,1024]{2,1,0:T(8,128)(2,1)S(1)} %pad_maximum_fusion.6), channel_id=1, source_target_pairs={{0,192},{1,25},{8,200},{9,1},{16,208},{17,9},{24,216},{25,17},{64,... | collective-permute-start | bytes 1572872 | tf_op jit(solution)/shard_map/ppermute | solution.py:39
  71.4 2.7 %collective-permute-start.16 = (bf16[4,64,1024]{2,1,0:T(8,128)(2,1)S(1)}, bf16[4,64,1024]{2,1,0:T(8,128)(2,1)S(1)}, u32[]{:S(2)}, u32[]{:S(2)}) collective-permute-start(bf16[4,64,1024]{2,1,0:T(8,128)(2,1)S(1)} %pad_maximum_fusion.3), channel_id=1, source_target_pairs={{0,192},{1,25},{8,200},{9,1},{16,208},{17,9},{24,216},{25,17},{64,... | collective-permute-start | bytes 1572872 | tf_op jit(solution)/shard_map/ppermute | solution.py:39
  74.1 2.6 %collective-permute-done.23 = bf16[4,64,1024]{2,1,0:T(8,128)(2,1)S(1)} collective-permute-done((bf16[4,64,1024]{2,1,0:T(8,128)(2,1)S(1)}, bf16[4,64,1024]{2,1,0:T(8,128)(2,1)S(1)}, u32[]{:S(2)}, u32[]{:S(2)}) %collective-permute-start.23) | collective-permute-done | bytes 524320 | tf_op jit(solution)/shard_map/ppermute | solution.py:39
  77.0 5.3 %collective-permute-done.14 = bf16[4,64,1024]{2,1,0:T(8,128)(2,1)S(1)} collective-permute-done((bf16[4,64,1024]{2,1,0:T(8,128)(2,1)S(1)}, bf16[4,64,1024]{2,1,0:T(8,128)(2,1)S(1)}, u32[]{:S(2)}, u32[]{:S(2)}) %collective-permute-start.14) | collective-permute-done | bytes 524320 | tf_op jit(solution)/shard_map/ppermute | solution.py:39
  82.7 1.6 collective-permute-start.26
  84.3 2.3 %collective-permute-start.27 = (bf16[128,1024]{1,0:T(8,128)(2,1)S(1)}, bf16[128,1024]{1,0:T(8,128)(2,1)S(1)}, u32[]{:S(2)}, u32[]{:S(2)}) collective-permute-start(bf16[128,1024]{1,0:T(8,128)(2,1)S(1)} %get-tuple-element.59), channel_id=1, source_target_pairs={{0,8},{1,65},{8,16},{9,73},{16,24},{17,81},{24,0},{25,89},{64,72},... | collective-permute-start | bytes 786440 | tf_op jit(solution)/shard_map/ppermute | solution.py:39
  87.0 2.9 %collective-permute-done.26 = bf16[128,1024]{1,0:T(8,128)(2,1)S(1)} collective-permute-done((bf16[128,1024]{1,0:T(8,128)(2,1)S(1)}, bf16[128,1024]{1,0:T(8,128)(2,1)S(1)}, u32[]{:S(2)}, u32[]{:S(2)}) %collective-permute-start.26) | collective-permute-done | bytes 262176 | tf_op jit(solution)/shard_map/ppermute | solution.py:39
  89.8 2.8 %collective-permute-done.27 = bf16[128,1024]{1,0:T(8,128)(2,1)S(1)} collective-permute-done((bf16[128,1024]{1,0:T(8,128)(2,1)S(1)}, bf16[128,1024]{1,0:T(8,128)(2,1)S(1)}, u32[]{:S(2)}, u32[]{:S(2)}) %collective-permute-start.27) | collective-permute-done | bytes 262176 | tf_op jit(solution)/shard_map/ppermute | solution.py:39
  93.7 14.0 %all_to_all.10.parts = bf16[8,16,1024]{2,1,0:T(8,128)(2,1)S(1)} all-to-all(bf16[8,16,1024]{2,1,0:T(8,128)(2,1)S(1)} %bitcast.61), channel_id=1, replica_groups=mesh['x'=4,'zl'=2,'y'=4,'zh'=4,'c'=2] {'zh','zl'}, dimensions={0} | all-to-all | bytes 524288 | tf_op jit(solution)/shard_map/all_to_all | solution.py:312
  108.2 11.9 %all_to_all.11 = bf16[8,16,1024]{2,1,0:T(8,128)(2,1)S(1)} all-to-all(bf16[8,16,1024]{2,1,0:T(8,128)(2,1)S(1)} %shard_map.89), channel_id=1, replica_groups=mesh['x'=4,'zl'=2,'y'=4,'zh'=4,'c'=2] {'zh','zl'}, dimensions={0} | all-to-all | bytes 524288 | tf_op jit(solution)/shard_map/all_to_all | solution.py:314
  120.8 2.3 %collective-permute-start.30 = (bf16[128,1024]{1,0:T(8,128)(2,1)S(1)}, bf16[128,1024]{1,0:T(8,128)(2,1)S(1)}, u32[]{:S(2)}, u32[]{:S(2)}) collective-permute-start(bf16[128,1024]{1,0:T(8,128)(2,1)S(1)} %bitcast.59), channel_id=1, source_target_pairs={{0,8},{1,65},{8,16},{9,73},{16,24},{17,81},{24,0},{25,89},{64,72},... | collective-permute-start | bytes 786440 | tf_op jit(solution)/shard_map/ppermute | solution.py:39
  123.5 3.5 %collective-permute-done.29 = bf16[128,1024]{1,0:T(8,128)(2,1)S(1)} collective-permute-done((bf16[128,1024]{1,0:T(8,128)(2,1)S(1)}, bf16[128,1024]{1,0:T(8,128)(2,1)S(1)}, u32[]{:S(2)}, u32[]{:S(2)}) %collective-permute-start.29) | collective-permute-done | bytes 262176 | tf_op jit(solution)/shard_map/ppermute | solution.py:39
  127.0 3.0 %collective-permute-done.30 = bf16[128,1024]{1,0:T(8,128)(2,1)S(1)} collective-permute-done((bf16[128,1024]{1,0:T(8,128)(2,1)S(1)}, bf16[128,1024]{1,0:T(8,128)(2,1)S(1)}, u32[]{:S(2)}, u32[]{:S(2)}) %collective-permute-start.30) | collective-permute-done | bytes 262176 | tf_op jit(solution)/shard_map/ppermute | solution.py:39
  131.1 2.5 %collective-permute-start.36 = (bf16[4,64,1024]{2,1,0:T(8,128)(2,1)S(1)}, bf16[4,64,1024]{2,1,0:T(8,128)(2,1)S(1)}, u32[]{:S(2)}, u32[]{:S(2)}) collective-permute-start(bf16[4,64,1024]{2,1,0:T(8,128)(2,1)S(1)} %pad_maximum_fusion.8.refs_0_), channel_id=1, source_target_pairs={{0,64},{1,9},{8,72},{9,17},{16,80},{17,25},{24,88},{25,1},{64,128}... | collective-permute-start | bytes 1572872 | tf_op jit(solution)/shard_map/ppermute | solution.py:39
  133.8 1.7 collective-permute-start.32
  135.6 5.2 %collective-permute-done.35.refs_1_ = bf16[4,64,1024]{2,1,0:T(8,128)(2,1)S(1)} collective-permute-done((bf16[4,64,1024]{2,1,0:T(8,128)(2,1)S(1)}, bf16[4,64,1024]{2,1,0:T(8,128)(2,1)S(1)}, u32[]{:S(2)}, u32[]{:S(2)}) %collective-permute-start.35) | collective-permute-done | bytes 524320 | tf_op jit(solution)/shard_map/ppermute | solution.py:39
  140.7 2.4 %collective-permute-start.34 = (bf16[4,64,1024]{2,1,0:T(8,128)(2,1)S(1)}, bf16[4,64,1024]{2,1,0:T(8,128)(2,1)S(1)}, u32[]{:S(2)}, u32[]{:S(2)}) collective-permute-start(bf16[4,64,1024]{2,1,0:T(8,128)(2,1)S(1)} %pad_maximum_fusion.7.refs_0_), channel_id=1, source_target_pairs={{0,192},{1,25},{8,200},{9,1},{16,208},{17,9},{24,216},{25,17},{64,... | collective-permute-start | bytes 1572872 | tf_op jit(solution)/shard_map/ppermute | solution.py:39
  143.1 3.1 %collective-permute-done.36.refs_2_ = bf16[4,64,1024]{2,1,0:T(8,128)(2,1)S(1)} collective-permute-done((bf16[4,64,1024]{2,1,0:T(8,128)(2,1)S(1)}, bf16[4,64,1024]{2,1,0:T(8,128)(2,1)S(1)}, u32[]{:S(2)}, u32[]{:S(2)}) %collective-permute-start.36) | collective-permute-done | bytes 524320 | tf_op jit(solution)/shard_map/ppermute | solution.py:39
  146.3 2.3 %shard_map.90 = (bf16[256,4096]{1,0:T(8,128)(2,1)S(1)}, f32[256,256]{1,0:T(8,128)S(1)}) custom-call(s32[4]{0:T(128)S(1)} %pad_add_fusion.me, bf16[256,4096]{1,0:T(8,128)(2,1)S(1)} %pad_maximum_fusion.weight, f32[1,4096]{1,0:T(1,128)S(1)} %bitcast.52, f32[1,256]{1,0:T(1,128)S(1)} %bitcast.56, bf16[4,64,1024]{2,1,0:T(8,128)(2,1)S(1)} %pad_maximum_fusion.8.refs_0_, ...), custom_call_target="tpu_custom_call" | custom-call | flops 536870912 | bytes 4194304 | tf_op jit(solution)/shard_map/pallas_call | solution.py:109
  148.6 13.9 %collective-permute-start.38 = (f32[256,256]{1,0:T(8,128)S(1)}, f32[256,256]{1,0:T(8,128)S(1)}, u32[]{:S(2)}, u32[]{:S(2)}) collective-permute-start(f32[256,256]{1,0:T(8,128)S(1)} %get-tuple-element.42.own), channel_id=1, source_target_pairs={{0,1},{1,0},{2,3},{3,2},{4,5},{5,4},{6,7},{7,6},{8,9},{9,8},{10,11... | collective-permute-start | bytes 786440 | tf_op jit(solution)/shard_map/ppermute | solution.py:43
  163.7 2.6 %shard_map.91.refs_4_.refs_0_ = f32[256,4096]{1,0:T(8,128)S(1)} custom-call(f32[256,256]{1,0:T(8,128)S(1)} %get-tuple-element.42.own, f32[256,256]{1,0:T(8,128)S(1)} %collective-permute-done.38.other, f32[256,256]{1,0:T(8,128)S(1)} %get-tuple-element.43.preact, bf16[256,256]{1,0:T(8,128)(2,1)S(1)} %get-tuple-element.44.flat, ...), custom_call_target="tpu_custom_call" | custom-call | flops 1073741824 | bytes 12582912 | tf_op jit(solution)/shard_map/pallas_call | solution.py:220
  166.2 1.7 shard_map.92
  167.9 5.2 %collective-permute-start.39 = (f32[256,256]{1,0:T(8,128)S(1)}, f32[256,256]{1,0:T(8,128)S(1)}, u32[]{:S(2)}, u32[]{:S(2)}) collective-permute-start(f32[256,256]{1,0:T(8,128)S(1)} %get-tuple-element.47.own), channel_id=1, source_target_pairs={{0,1},{1,0},{2,3},{3,2},{4,5},{5,4},{6,7},{7,6},{8,9},{9,8},{10,11... | collective-permute-start | bytes 786440 | tf_op jit(solution)/shard_map/ppermute | solution.py:43
  174.3 1.9 %shard_map.93 = (f32[128,4096]{1,0:T(8,128)S(1)}, bf16[128,4096]{1,0:T(8,128)(2,1)S(1)}) custom-call(f32[256,256]{1,0:T(8,128)S(1)} %get-tuple-element.47.own, f32[256,256]{1,0:T(8,128)S(1)} %collective-permute-done.39.other, f32[256,256]{1,0:T(8,128)S(1)} %get-tuple-element.48.preact, bf16[256,256]{1,0:T(8,128)(2,1)S(1)} %get-tuple-element.49.flat, ...), custom_call_target="tpu_custom_call" | custom-call | flops 1073741824 | bytes 12582912 | tf_op jit(solution)/shard_map/pallas_call | solution.py:220
  176.7 3.5 %shard_map.94 = (bf16[128,8192]{1,0:T(8,128)(2,1)}, bf16[128,8192]{1,0:T(8,128)(2,1)}, bf16[128,8192]{1,0:T(8,128)(2,1)}) custom-call(s32[1]{0:T(128)} %bitcast.at, f32[128,4096]{1,0:T(8,128)S(1)} %get-tuple-element.53.gradient_ref, bf16[128,8192]{1,0:T(8,128)(2,1)S(1)} %copy-done, bf16[128,8192]{1,0:T(8,128)(2,1)S(1)} %copy-done.1), custom_call_target="tpu_custom_call" | custom-call | flops 10485760 | bytes 7340032 | tf_op jit(solution)/shard_map/pallas_call | solution.py:255
  180.2 3.6 %shard_map.95 = (bf16[128,8192]{1,0:T(8,128)(2,1)}, bf16[128,8192]{1,0:T(8,128)(2,1)}, bf16[128,8192]{1,0:T(8,128)(2,1)}) custom-call(s32[1]{0:T(128)S(6)} %sub.15.at, bf16[128,4096]{1,0:T(8,128)(2,1)S(1)} %collective-permute-done.40.gradient_ref, bf16[128,8192]{1,0:T(8,128)(2,1)S(1)} %copy-done, ...), custom_call_target="tpu_custom_call", output_to_operand_aliasing={{0}: (4, {}), {1}: (5, {}), {2}: (6, {})} | custom-call | flops 10485760 | bytes 7340032 | tf_op jit(solution)/shard_map/pallas_call | solution.py:255
  (96 shorter events, 19.5 us)
Async XLA Ops:
  1.4 4.1 %collective-permute-start.1 = (bf16[16,1024]{1,0:T(8,128)(2,1)S(1)}, bf16[16,1024]{1,0:T(8,128)(2,1)S(1)}, u32[]{:S(2)}, u32[]{:S(2)}) collective-permute-start(bf16[16,1024]{1,0:T(8,128)(2,1)S(1)} %constant_dynamic-slice_fusion), channel_id=1, source_target_pairs={{0,1},{1,0},{2,3},{3,2},{4,5},{5,4},{6,7},{7,6},{8,9},{9,8},{10,11... | collective-permute-start | bytes 98312 | tf_op jit(solution)/shard_map/ppermute | solution.py:43
  6.3 9.5 %collective-permute-start.2 = (bf16[32,1024]{1,0:T(8,128)(2,1)S(1)}, bf16[32,1024]{1,0:T(8,128)(2,1)S(1)}, u32[]{:S(2)}, u32[]{:S(2)}) collective-permute-start(bf16[32,1024]{1,0:T(8,128)(2,1)S(1)} %get-tuple-element.86), channel_id=1, source_target_pairs={{0,4},{2,6},{4,0},{6,2},{1,5},{3,7},{5,1},{7,3},{8,12},{10,14},{12... | collective-permute-start | bytes 196616 | tf_op jit(solution)/shard_map/ppermute | solution.py:285
  11.6 35.8 %collective-permute-start = (bf16[128,8192]{1,0:T(8,128)(2,1)}, bf16[128,8192]{1,0:T(8,128)(2,1)}, u32[]{:S(2)}, u32[]{:S(2)}) collective-permute-start(bf16[128,8192]{1,0:T(8,128)(2,1)} %param.8), channel_id=1, source_target_pairs={{0,1},{1,0},{2,3},{3,2},{4,5},{5,4},{6,7},{7,6},{8,9},{9,8},{10,11... | collective-permute-start | bytes 6291464 | tf_op jit(solution)/shard_map/ppermute | solution.py:43
  12.2 6.6 %collective-permute-start.3 = (bf16[32,1024]{1,0:T(8,128)(2,1)S(1)}, bf16[32,1024]{1,0:T(8,128)(2,1)S(1)}, u32[]{:S(2)}, u32[]{:S(2)}) collective-permute-start(bf16[32,1024]{1,0:T(8,128)(2,1)S(1)} %get-tuple-element.86), channel_id=1, source_target_pairs={{0,2},{2,4},{4,6},{6,0},{1,3},{3,5},{5,7},{7,1},{8,10},{10,12},{12... | collective-permute-start | bytes 196616 | tf_op jit(solution)/shard_map/ppermute | solution.py:285
  13.4 5.4 %collective-permute-start.4 = (bf16[32,1024]{1,0:T(8,128)(2,1)S(1)}, bf16[32,1024]{1,0:T(8,128)(2,1)S(1)}, u32[]{:S(2)}, u32[]{:S(2)}) collective-permute-start(bf16[32,1024]{1,0:T(8,128)(2,1)S(1)} %get-tuple-element.86), channel_id=1, source_target_pairs={{0,6},{2,0},{4,2},{6,4},{1,7},{3,1},{5,3},{7,5},{8,14},{10,8},{12,... | collective-permute-start | bytes 196616 | tf_op jit(solution)/shard_map/ppermute | solution.py:285
  18.9 7.1 %collective-permute-start.5 = (bf16[128,1024]{1,0:T(8,128)(2,1)S(1)}, bf16[128,1024]{1,0:T(8,128)(2,1)S(1)}, u32[]{:S(2)}, u32[]{:S(2)}) collective-permute-start(bf16[128,1024]{1,0:T(8,128)(2,1)S(1)} %constant_dynamic-update-slice_fusion.source), channel_id=1, source_target_pairs={{0,16},{1,129},{8,24},{9,137},{16,0},{17,145},{24,8},{25,153},{64,... | collective-permute-start | bytes 786440 | tf_op jit(solution)/shard_map/ppermute | solution.py:39
  21.7 13.1 %copy-start.2 = (f32[8192]{0:T(1024)S(1)}, f32[8192]{0:T(1024)}, u32[]{:S(2)}) copy-start(f32[8192]{0:T(1024)} %param.7) | copy-start | bytes 98308
  21.7 13.1 %copy-start.3 = (f32[128]{0:T(128)S(1)}, f32[128]{0:T(128)}, u32[]{:S(2)}) copy-start(f32[128]{0:T(128)} %param.9) | copy-start | bytes 1540
  21.7 7.1 %collective-permute-start.6 = (bf16[128,1024]{1,0:T(8,128)(2,1)S(1)}, bf16[128,1024]{1,0:T(8,128)(2,1)S(1)}, u32[]{:S(2)}, u32[]{:S(2)}) collective-permute-start(bf16[128,1024]{1,0:T(8,128)(2,1)S(1)} %constant_dynamic-update-slice_fusion.source), channel_id=1, source_target_pairs={{0,8},{1,65},{8,16},{9,73},{16,24},{17,81},{24,0},{25,89},{64,72},... | collective-permute-start | bytes 786440 | tf_op jit(solution)/shard_map/ppermute | solution.py:39
  22.0 6.9 %collective-permute-start.7 = (bf16[128,1024]{1,0:T(8,128)(2,1)S(1)}, bf16[128,1024]{1,0:T(8,128)(2,1)S(1)}, u32[]{:S(2)}, u32[]{:S(2)}) collective-permute-start(bf16[128,1024]{1,0:T(8,128)(2,1)S(1)} %constant_dynamic-update-slice_fusion.source), channel_id=1, source_target_pairs={{0,24},{1,193},{8,0},{9,201},{16,8},{17,209},{24,16},{25,217},{64,... | collective-permute-start | bytes 786440 | tf_op jit(solution)/shard_map/ppermute | solution.py:39
  29.0 9.7 %collective-permute-start.17 = (bf16[4,64,1024]{2,1,0:T(8,128)(2,1)S(1)}, bf16[4,64,1024]{2,1,0:T(8,128)(2,1)S(1)}, u32[]{:S(2)}, u32[]{:S(2)}) collective-permute-start(bf16[4,64,1024]{2,1,0:T(8,128)(2,1)S(1)} %pad_maximum_fusion.4.refs_0_), channel_id=1, source_target_pairs={{0,64},{1,9},{8,72},{9,17},{16,80},{17,25},{24,88},{25,1},{64,128}... | collective-permute-start | bytes 1572872 | tf_op jit(solution)/shard_map/ppermute | solution.py:39
  30.4 8.4 %collective-permute-start.18 = (bf16[4,64,1024]{2,1,0:T(8,128)(2,1)S(1)}, bf16[4,64,1024]{2,1,0:T(8,128)(2,1)S(1)}, u32[]{:S(2)}, u32[]{:S(2)}) collective-permute-start(bf16[4,64,1024]{2,1,0:T(8,128)(2,1)S(1)} %pad_maximum_fusion.4.refs_0_), channel_id=1, source_target_pairs={{0,192},{1,25},{8,200},{9,1},{16,208},{17,9},{24,216},{25,17},{64,... | collective-permute-start | bytes 1572872 | tf_op jit(solution)/shard_map/ppermute | solution.py:39
  32.0 12.3 %collective-permute-start.8 = (bf16[4,64,1024]{2,1,0:T(8,128)(2,1)S(1)}, bf16[4,64,1024]{2,1,0:T(8,128)(2,1)S(1)}, u32[]{:S(2)}, u32[]{:S(2)}) collective-permute-start(bf16[4,64,1024]{2,1,0:T(8,128)(2,1)S(1)} %pad_maximum_fusion.1.refs_0_), channel_id=1, source_target_pairs={{0,64},{1,9},{8,72},{9,17},{16,80},{17,25},{24,88},{25,1},{64,128}... | collective-permute-start | bytes 1572872 | tf_op jit(solution)/shard_map/ppermute | solution.py:39
  32.1 12.4 %collective-permute-start.9 = (bf16[4,64,1024]{2,1,0:T(8,128)(2,1)S(1)}, bf16[4,64,1024]{2,1,0:T(8,128)(2,1)S(1)}, u32[]{:S(2)}, u32[]{:S(2)}) collective-permute-start(bf16[4,64,1024]{2,1,0:T(8,128)(2,1)S(1)} %pad_maximum_fusion.1.refs_0_), channel_id=1, source_target_pairs={{0,192},{1,25},{8,200},{9,1},{16,208},{17,9},{24,216},{25,17},{64,... | collective-permute-start | bytes 1572872 | tf_op jit(solution)/shard_map/ppermute | solution.py:39
  38.7 10.2 %collective-permute-start.19 = (bf16[2,64,1024]{2,1,0:T(8,128)(2,1)S(1)}, bf16[2,64,1024]{2,1,0:T(8,128)(2,1)S(1)}, u32[]{:S(2)}, u32[]{:S(2)}) collective-permute-start(bf16[2,64,1024]{2,1,0:T(8,128)(2,1)S(1)} %slice.140), channel_id=1, source_target_pairs={{0,64},{1,9},{8,72},{9,17},{16,80},{17,25},{24,88},{25,1},{64,128}... | collective-permute-start | bytes 786440 | tf_op jit(solution)/shard_map/ppermute | solution.py:39
  38.8 10.1 %collective-permute-start.20 = (bf16[2,64,1024]{2,1,0:T(8,128)(2,1)S(1)}, bf16[2,64,1024]{2,1,0:T(8,128)(2,1)S(1)}, u32[]{:S(2)}, u32[]{:S(2)}) collective-permute-start(bf16[2,64,1024]{2,1,0:T(8,128)(2,1)S(1)} %slice.141), channel_id=1, source_target_pairs={{0,192},{1,25},{8,200},{9,1},{16,208},{17,9},{24,216},{25,17},{64,... | collective-permute-start | bytes 786440 | tf_op jit(solution)/shard_map/ppermute | solution.py:39
  44.3 10.5 %collective-permute-start.10 = (bf16[2,64,1024]{2,1,0:T(8,128)(2,1)S(1)}, bf16[2,64,1024]{2,1,0:T(8,128)(2,1)S(1)}, u32[]{:S(2)}, u32[]{:S(2)}) collective-permute-start(bf16[2,64,1024]{2,1,0:T(8,128)(2,1)S(1)} %slice.134), channel_id=1, source_target_pairs={{0,64},{1,9},{8,72},{9,17},{16,80},{17,25},{24,88},{25,1},{64,128}... | collective-permute-start | bytes 786440 | tf_op jit(solution)/shard_map/ppermute | solution.py:39
  44.4 10.3 %collective-permute-start.11 = (bf16[2,64,1024]{2,1,0:T(8,128)(2,1)S(1)}, bf16[2,64,1024]{2,1,0:T(8,128)(2,1)S(1)}, u32[]{:S(2)}, u32[]{:S(2)}) collective-permute-start(bf16[2,64,1024]{2,1,0:T(8,128)(2,1)S(1)} %slice.135), channel_id=1, source_target_pairs={{0,192},{1,25},{8,200},{9,1},{16,208},{17,9},{24,216},{25,17},{64,... | collective-permute-start | bytes 786440 | tf_op jit(solution)/shard_map/ppermute | solution.py:39
  50.8 6.5 %collective-permute-start.21 = (f32[256,256]{1,0:T(8,128)S(1)}, f32[256,256]{1,0:T(8,128)S(1)}, u32[]{:S(2)}, u32[]{:S(2)}) collective-permute-start(f32[256,256]{1,0:T(8,128)S(1)} %get-tuple-element.36.own), channel_id=1, source_target_pairs={{0,1},{1,0},{2,3},{3,2},{4,5},{5,4},{6,7},{7,6},{8,9},{9,8},{10,11... | collective-permute-start | bytes 786440 | tf_op jit(solution)/shard_map/ppermute | solution.py:43
  56.7 5.9 %collective-permute-start.12 = (f32[256,256]{1,0:T(8,128)S(1)}, f32[256,256]{1,0:T(8,128)S(1)}, u32[]{:S(2)}, u32[]{:S(2)}) collective-permute-start(f32[256,256]{1,0:T(8,128)S(1)} %get-tuple-element.30.own), channel_id=1, source_target_pairs={{0,1},{1,0},{2,3},{3,2},{4,5},{5,4},{6,7},{7,6},{8,9},{9,8},{10,11... | collective-permute-start | bytes 786440 | tf_op jit(solution)/shard_map/ppermute | solution.py:43
  59.6 7.4 %collective-permute-start.22 = (bf16[2,64,1024]{2,1,0:T(8,128)(2,1)S(1)}, bf16[2,64,1024]{2,1,0:T(8,128)(2,1)S(1)}, u32[]{:S(2)}, u32[]{:S(2)}) collective-permute-start(bf16[2,64,1024]{2,1,0:T(8,128)(2,1)S(1)} %get-tuple-element.39), channel_id=1, source_target_pairs={{0,64},{1,9},{8,72},{9,17},{16,80},{17,25},{24,88},{25,1},{64,128}... | collective-permute-start | bytes 786440 | tf_op jit(solution)/shard_map/ppermute | solution.py:39
  60.9 6.3 %collective-permute-start.24 = (bf16[2,64,1024]{2,1,0:T(8,128)(2,1)S(1)}, bf16[2,64,1024]{2,1,0:T(8,128)(2,1)S(1)}, u32[]{:S(2)}, u32[]{:S(2)}) collective-permute-start(bf16[2,64,1024]{2,1,0:T(8,128)(2,1)S(1)} %get-tuple-element.41), channel_id=1, source_target_pairs={{0,192},{1,25},{8,200},{9,1},{16,208},{17,9},{24,216},{25,17},{64,... | collective-permute-start | bytes 786440 | tf_op jit(solution)/shard_map/ppermute | solution.py:39
  64.2 6.8 %collective-permute-start.13 = (bf16[2,64,1024]{2,1,0:T(8,128)(2,1)S(1)}, bf16[2,64,1024]{2,1,0:T(8,128)(2,1)S(1)}, u32[]{:S(2)}, u32[]{:S(2)}) collective-permute-start(bf16[2,64,1024]{2,1,0:T(8,128)(2,1)S(1)} %get-tuple-element.33), channel_id=1, source_target_pairs={{0,64},{1,9},{8,72},{9,17},{16,80},{17,25},{24,88},{25,1},{64,128}... | collective-permute-start | bytes 786440 | tf_op jit(solution)/shard_map/ppermute | solution.py:39
  64.3 6.9 %collective-permute-start.15 = (bf16[2,64,1024]{2,1,0:T(8,128)(2,1)S(1)}, bf16[2,64,1024]{2,1,0:T(8,128)(2,1)S(1)}, u32[]{:S(2)}, u32[]{:S(2)}) collective-permute-start(bf16[2,64,1024]{2,1,0:T(8,128)(2,1)S(1)} %get-tuple-element.35), channel_id=1, source_target_pairs={{0,192},{1,25},{8,200},{9,1},{16,208},{17,9},{24,216},{25,17},{64,... | collective-permute-start | bytes 786440 | tf_op jit(solution)/shard_map/ppermute | solution.py:39
  67.1 9.6 %collective-permute-start.23 = (bf16[4,64,1024]{2,1,0:T(8,128)(2,1)S(1)}, bf16[4,64,1024]{2,1,0:T(8,128)(2,1)S(1)}, u32[]{:S(2)}, u32[]{:S(2)}) collective-permute-start(bf16[4,64,1024]{2,1,0:T(8,128)(2,1)S(1)} %pad_maximum_fusion.5), channel_id=1, source_target_pairs={{0,64},{1,9},{8,72},{9,17},{16,80},{17,25},{24,88},{25,1},{64,128}... | collective-permute-start | bytes 1572872 | tf_op jit(solution)/shard_map/ppermute | solution.py:39
  67.3 9.4 %collective-permute-start.25 = (bf16[4,64,1024]{2,1,0:T(8,128)(2,1)S(1)}, bf16[4,64,1024]{2,1,0:T(8,128)(2,1)S(1)}, u32[]{:S(2)}, u32[]{:S(2)}) collective-permute-start(bf16[4,64,1024]{2,1,0:T(8,128)(2,1)S(1)} %pad_maximum_fusion.6), channel_id=1, source_target_pairs={{0,192},{1,25},{8,200},{9,1},{16,208},{17,9},{24,216},{25,17},{64,... | collective-permute-start | bytes 1572872 | tf_op jit(solution)/shard_map/ppermute | solution.py:39
  71.2 11.2 %collective-permute-start.14 = (bf16[4,64,1024]{2,1,0:T(8,128)(2,1)S(1)}, bf16[4,64,1024]{2,1,0:T(8,128)(2,1)S(1)}, u32[]{:S(2)}, u32[]{:S(2)}) collective-permute-start(bf16[4,64,1024]{2,1,0:T(8,128)(2,1)S(1)} %pad_maximum_fusion.2), channel_id=1, source_target_pairs={{0,64},{1,9},{8,72},{9,17},{16,80},{17,25},{24,88},{25,1},{64,128}... | collective-permute-start | bytes 1572872 | tf_op jit(solution)/shard_map/ppermute | solution.py:39
  71.4 11.0 %collective-permute-start.16 = (bf16[4,64,1024]{2,1,0:T(8,128)(2,1)S(1)}, bf16[4,64,1024]{2,1,0:T(8,128)(2,1)S(1)}, u32[]{:S(2)}, u32[]{:S(2)}) collective-permute-start(bf16[4,64,1024]{2,1,0:T(8,128)(2,1)S(1)} %pad_maximum_fusion.3), channel_id=1, source_target_pairs={{0,192},{1,25},{8,200},{9,1},{16,208},{17,9},{24,216},{25,17},{64,... | collective-permute-start | bytes 1572872 | tf_op jit(solution)/shard_map/ppermute | solution.py:39
  82.7 7.1 %collective-permute-start.26 = (bf16[128,1024]{1,0:T(8,128)(2,1)S(1)}, bf16[128,1024]{1,0:T(8,128)(2,1)S(1)}, u32[]{:S(2)}, u32[]{:S(2)}) collective-permute-start(bf16[128,1024]{1,0:T(8,128)(2,1)S(1)} %get-tuple-element.57), channel_id=1, source_target_pairs={{0,16},{1,129},{8,24},{9,137},{16,0},{17,145},{24,8},{25,153},{64,... | collective-permute-start | bytes 786440 | tf_op jit(solution)/shard_map/ppermute | solution.py:39
  84.3 8.3 %collective-permute-start.27 = (bf16[128,1024]{1,0:T(8,128)(2,1)S(1)}, bf16[128,1024]{1,0:T(8,128)(2,1)S(1)}, u32[]{:S(2)}, u32[]{:S(2)}) collective-permute-start(bf16[128,1024]{1,0:T(8,128)(2,1)S(1)} %get-tuple-element.59), channel_id=1, source_target_pairs={{0,8},{1,65},{8,16},{9,73},{16,24},{17,81},{24,0},{25,89},{64,72},... | collective-permute-start | bytes 786440 | tf_op jit(solution)/shard_map/ppermute | solution.py:39
  86.6 6.9 %collective-permute-start.28 = (bf16[128,1024]{1,0:T(8,128)(2,1)S(1)}, bf16[128,1024]{1,0:T(8,128)(2,1)S(1)}, u32[]{:S(2)}, u32[]{:S(2)}) collective-permute-start(bf16[128,1024]{1,0:T(8,128)(2,1)S(1)} %get-tuple-element.58), channel_id=1, source_target_pairs={{0,24},{1,193},{8,0},{9,201},{16,8},{17,209},{24,16},{25,217},{64,... | collective-permute-start | bytes 786440 | tf_op jit(solution)/shard_map/ppermute | solution.py:39
  120.1 6.8 %collective-permute-start.29 = (bf16[128,1024]{1,0:T(8,128)(2,1)S(1)}, bf16[128,1024]{1,0:T(8,128)(2,1)S(1)}, u32[]{:S(2)}, u32[]{:S(2)}) collective-permute-start(bf16[128,1024]{1,0:T(8,128)(2,1)S(1)} %bitcast.58), channel_id=1, source_target_pairs={{0,16},{1,129},{8,24},{9,137},{16,0},{17,145},{24,8},{25,153},{64,... | collective-permute-start | bytes 786440 | tf_op jit(solution)/shard_map/ppermute | solution.py:39
  120.8 9.2 %collective-permute-start.30 = (bf16[128,1024]{1,0:T(8,128)(2,1)S(1)}, bf16[128,1024]{1,0:T(8,128)(2,1)S(1)}, u32[]{:S(2)}, u32[]{:S(2)}) collective-permute-start(bf16[128,1024]{1,0:T(8,128)(2,1)S(1)} %bitcast.59), channel_id=1, source_target_pairs={{0,8},{1,65},{8,16},{9,73},{16,24},{17,81},{24,0},{25,89},{64,72},... | collective-permute-start | bytes 786440 | tf_op jit(solution)/shard_map/ppermute | solution.py:39
  123.1 6.9 %collective-permute-start.31 = (bf16[128,1024]{1,0:T(8,128)(2,1)S(1)}, bf16[128,1024]{1,0:T(8,128)(2,1)S(1)}, u32[]{:S(2)}, u32[]{:S(2)}) collective-permute-start(bf16[128,1024]{1,0:T(8,128)(2,1)S(1)} %bitcast.60), channel_id=1, source_target_pairs={{0,24},{1,193},{8,0},{9,201},{16,8},{17,209},{24,16},{25,217},{64,... | collective-permute-start | bytes 786440 | tf_op jit(solution)/shard_map/ppermute | solution.py:39
  130.1 10.6 %collective-permute-start.35 = (bf16[4,64,1024]{2,1,0:T(8,128)(2,1)S(1)}, bf16[4,64,1024]{2,1,0:T(8,128)(2,1)S(1)}, u32[]{:S(2)}, u32[]{:S(2)}) collective-permute-start(bf16[4,64,1024]{2,1,0:T(8,128)(2,1)S(1)} %pad_maximum_fusion.8.refs_0_), channel_id=1, source_target_pairs={{0,128},{1,17},{8,136},{9,25},{16,144},{17,1},{24,152},{25,9},{64,... | collective-permute-start | bytes 1572872 | tf_op jit(solution)/shard_map/ppermute | solution.py:39
  131.1 15.1 %collective-permute-start.36 = (bf16[4,64,1024]{2,1,0:T(8,128)(2,1)S(1)}, bf16[4,64,1024]{2,1,0:T(8,128)(2,1)S(1)}, u32[]{:S(2)}, u32[]{:S(2)}) collective-permute-start(bf16[4,64,1024]{2,1,0:T(8,128)(2,1)S(1)} %pad_maximum_fusion.8.refs_0_), channel_id=1, source_target_pairs={{0,64},{1,9},{8,72},{9,17},{16,80},{17,25},{24,88},{25,1},{64,128}... | collective-permute-start | bytes 1572872 | tf_op jit(solution)/shard_map/ppermute | solution.py:39
  133.6 12.7 %collective-permute-start.37 = (bf16[4,64,1024]{2,1,0:T(8,128)(2,1)S(1)}, bf16[4,64,1024]{2,1,0:T(8,128)(2,1)S(1)}, u32[]{:S(2)}, u32[]{:S(2)}) collective-permute-start(bf16[4,64,1024]{2,1,0:T(8,128)(2,1)S(1)} %pad_maximum_fusion.8.refs_0_), channel_id=1, source_target_pairs={{0,192},{1,25},{8,200},{9,1},{16,208},{17,9},{24,216},{25,17},{64,... | collective-permute-start | bytes 1572872 | tf_op jit(solution)/shard_map/ppermute | solution.py:39
  133.8 32.4 %collective-permute-start.32 = (bf16[4,64,1024]{2,1,0:T(8,128)(2,1)S(1)}, bf16[4,64,1024]{2,1,0:T(8,128)(2,1)S(1)}, u32[]{:S(2)}, u32[]{:S(2)}) collective-permute-start(bf16[4,64,1024]{2,1,0:T(8,128)(2,1)S(1)} %pad_maximum_fusion.7.refs_0_), channel_id=1, source_target_pairs={{0,128},{1,17},{8,136},{9,25},{16,144},{17,1},{24,152},{25,9},{64,... | collective-permute-start | bytes 1572872 | tf_op jit(solution)/shard_map/ppermute | solution.py:39
  135.5 30.7 %collective-permute-start.33 = (bf16[4,64,1024]{2,1,0:T(8,128)(2,1)S(1)}, bf16[4,64,1024]{2,1,0:T(8,128)(2,1)S(1)}, u32[]{:S(2)}, u32[]{:S(2)}) collective-permute-start(bf16[4,64,1024]{2,1,0:T(8,128)(2,1)S(1)} %pad_maximum_fusion.7.refs_0_), channel_id=1, source_target_pairs={{0,64},{1,9},{8,72},{9,17},{16,80},{17,25},{24,88},{25,1},{64,128}... | collective-permute-start | bytes 1572872 | tf_op jit(solution)/shard_map/ppermute | solution.py:39
  140.7 25.5 %collective-permute-start.34 = (bf16[4,64,1024]{2,1,0:T(8,128)(2,1)S(1)}, bf16[4,64,1024]{2,1,0:T(8,128)(2,1)S(1)}, u32[]{:S(2)}, u32[]{:S(2)}) collective-permute-start(bf16[4,64,1024]{2,1,0:T(8,128)(2,1)S(1)} %pad_maximum_fusion.7.refs_0_), channel_id=1, source_target_pairs={{0,192},{1,25},{8,200},{9,1},{16,208},{17,9},{24,216},{25,17},{64,... | collective-permute-start | bytes 1572872 | tf_op jit(solution)/shard_map/ppermute | solution.py:39
  148.6 15.1 %collective-permute-start.38 = (f32[256,256]{1,0:T(8,128)S(1)}, f32[256,256]{1,0:T(8,128)S(1)}, u32[]{:S(2)}, u32[]{:S(2)}) collective-permute-start(f32[256,256]{1,0:T(8,128)S(1)} %get-tuple-element.42.own), channel_id=1, source_target_pairs={{0,1},{1,0},{2,3},{3,2},{4,5},{5,4},{6,7},{7,6},{8,9},{9,8},{10,11... | collective-permute-start | bytes 786440 | tf_op jit(solution)/shard_map/ppermute | solution.py:43
  167.9 6.4 %collective-permute-start.39 = (f32[256,256]{1,0:T(8,128)S(1)}, f32[256,256]{1,0:T(8,128)S(1)}, u32[]{:S(2)}, u32[]{:S(2)}) collective-permute-start(f32[256,256]{1,0:T(8,128)S(1)} %get-tuple-element.47.own), channel_id=1, source_target_pairs={{0,1},{1,0},{2,3},{3,2},{4,5},{5,4},{6,7},{7,6},{8,9},{9,8},{10,11... | collective-permute-start | bytes 786440 | tf_op jit(solution)/shard_map/ppermute | solution.py:43
  174.3 2.3 %copy-start = (bf16[128,8192]{1,0:T(8,128)(2,1)S(1)}, bf16[128,8192]{1,0:T(8,128)(2,1)}, u32[]{:S(2)}) copy-start(bf16[128,8192]{1,0:T(8,128)(2,1)} %first_ref.3) | copy-start | bytes 6291460
  174.3 2.3 %copy-start.1 = (bf16[128,8192]{1,0:T(8,128)(2,1)S(1)}, bf16[128,8192]{1,0:T(8,128)(2,1)}, u32[]{:S(2)}) copy-start(bf16[128,8192]{1,0:T(8,128)(2,1)} %second_ref.3) | copy-start | bytes 6291460
  176.2 4.0 %collective-permute-start.40 = (bf16[128,4096]{1,0:T(8,128)(2,1)S(1)}, bf16[128,4096]{1,0:T(8,128)(2,1)S(1)}, u32[]{:S(2)}, u32[]{:S(2)}) collective-permute-start(bf16[128,4096]{1,0:T(8,128)(2,1)S(1)} %get-tuple-element.52), channel_id=1, source_target_pairs={{0,1},{1,0},{2,3},{3,2},{4,5},{5,4},{6,7},{7,6},{8,9},{9,8},{10,11... | collective-permute-start | bytes 3145736 | tf_op jit(solution)/shard_map/ppermute | solution.py:43
